TPU v7x, 128 devices: a whole 4x4x4 slice. The times are simulated.
128 devices in a mesh: dp: 8 (over x_hi, y), tensor: 16 (over z, x_lo, core).
Axes of the slice: x: 4 (x_hi: 2, x_lo: 2; x = x_hi * 2 + x_lo), y: 4, z: 4, core: 2. Of those that a mesh axis runs over, the one named last changes fastest.
Arguments:
- qkv_weight: bfloat16 [5120, 3584], P(('dp', 'tensor')), may hold values from -0.078125 to 0.078125
- out_weight: bfloat16 [2560, 5120], P(('dp', 'tensor')), may hold values from -0.125 to 0.125
- qkv_grad: bfloat16 [5120, 3584], P(('dp', 'tensor')), may hold values from -6 to 6
- out_grad: bfloat16 [2560, 5120], P(('dp', 'tensor')), may hold values from -6 to 6
- qkv_moment: float32 [5120, 3584], P(('dp', 'tensor')), may hold values from -2 to 2
- out_moment: float32 [2560, 5120], P(('dp', 'tensor')), may hold values from -2 to 2
- qkv_second: float32 [5120, 3584], P(('dp', 'tensor')), may hold values from 0.05 to 2
- out_second: float32 [2560, 5120], P(('dp', 'tensor')), may hold values from 0.05 to 2
- step_states: bfloat16 [4, 3072, 5120], P(None, 'dp', 'tensor'), may hold values from -6 to 6
- key_cache: bfloat16 [3072, 4, 320, 128], P(('dp', 'tensor')), may hold values from -1200 to 1200
- value_cache: bfloat16 [3072, 4, 320, 128], P(('dp', 'tensor')), may hold values from -6 to 6
- prompt_lengths: int32 [3072], P(('dp', 'tensor')), may hold values from 40 to 320, as said below
Outputs:
- qkv_updated: bfloat16 [5120, 3584], P(('dp', 'tensor'))
- out_updated: bfloat16 [2560, 5120], P(('dp', 'tensor'))
- qkv_moment_next: float32 [5120, 3584], P(('dp', 'tensor'))
- out_moment_next: float32 [2560, 5120], P(('dp', 'tensor'))
- qkv_second_next: float32 [5120, 3584], P(('dp', 'tensor'))
- out_second_next: float32 [2560, 5120], P(('dp', 'tensor'))
- step_outputs: bfloat16 [4, 3072, 5120], P(None, 'dp', 'tensor')
Inputs may be any that keep to these rules, and one draw needn't show every extreme that they name: Prompt b's cache holds valid entries at positions below prompt_lengths[b]; some prompt fills all 320 positions.
All inputs are finite; a program needn't handle non-finite values.
Results may differ from a plain program's by a relative error of at most 0.0045.
The roundings to bfloat16 on the way count: a program that leaves them out, or rounds other values in their place, can miss the bound.
Values may be sent and summed in bfloat16 or wider, within the bound.
No kernel may reach another device: no remote copies, remote signals or barrier semaphores. Data moves between devices by JAX's collectives and lax.ppermute only.
A program may use at most 128 MiB of HBM per device.

v0:
```python
import jax
import jax.numpy as jnp
from jax import lax
from jax.experimental import pallas as pl
from jax.experimental.pallas import tpu as pltpu
from jax.sharding import Mesh
from jax.sharding import PartitionSpec as P

D = 5120
HEADS = 20
KV_HEADS = 4
HEAD_DIM = 128
STEPS = 4
GROUP = HEADS // KV_HEADS
ATT = HEADS * HEAD_DIM
KV = KV_HEADS * HEAD_DIM
QKV = ATT + 2 * KV
PROMPT_DEV = 24
CACHE = 320
ROWS = STEPS * PROMPT_DEV
QKV_COLS = QKV // 4
OUT_COLS = D // 4
FEATURES = D // 16

beta_first = 0.9
beta_second = 0.95
learning_rate = 0.002
weight_decay = 0.1
adam_epsilon = 1e-08
bias_first = 1.0 - 0.9**10
bias_second = 1.0 - 0.95**10
norm_epsilon = 1e-06
rope_base = 1000000.0

SIZES = (2, 4, 4, 2, 2)
AXES = ("xh", "y", "z", "xl", "c")


def adam_update(param, grad, moment, second):
    param_wide = param.astype(jnp.float32)
    grad_wide = grad.astype(jnp.float32)
    moment_next = beta_first * moment + (1.0 - beta_first) * grad_wide
    second_next = beta_second * second + (1.0 - beta_second) * grad_wide * grad_wide
    moment_hat = moment_next / bias_first
    second_hat = second_next / bias_second
    updated = param_wide - learning_rate * (
        moment_hat / (jnp.sqrt(second_hat) + adam_epsilon) + weight_decay * param_wide
    )
    return (updated.astype(jnp.bfloat16), moment_next, second_next)


def device_of(x, y, z, c):
    return ((((x // 2) * 4 + y) * 4 + z) * 2 + x % 2) * 2 + c


def plane_pairs(phase, shift):
    pairs = []
    for x in range(4):
        for y in range(4):
            for z in range(4):
                for c in range(2):
                    if c == phase:
                        target = device_of((x + shift) % 4, y, z, c)
                    else:
                        target = device_of(x, (y + shift) % 4, z, c)
                    pairs.append((device_of(x, y, z, c), target))
    return pairs


def plane_permute(array, phase, shift):
    return lax.ppermute(array, AXES, plane_pairs(phase, shift))


def z_permute(array, shift):
    return lax.ppermute(array, "z", [(j, (j + shift) % 4) for j in range(4)])


def core_permute(array):
    return lax.ppermute(array, "c", [(0, 1), (1, 0)])


def z_ring(low, high):
    low_1, high_3 = z_permute(low, 1), z_permute(high, -1)
    high_1, low_3 = z_permute(high, 1), z_permute(low, -1)
    low_2, high_2 = z_permute(low_1, 1), z_permute(high_3, -1)
    return (low_1, low_2, low_3), (high_1, high_2, high_3)


def plane_gather(block):
    first = jnp.stack(
        [
            block,
            plane_permute(block, 0, 1),
            plane_permute(block, 0, 2),
            plane_permute(block, 0, -1),
        ]
    )
    return (first,) + tuple(plane_permute(first, 1, shift) for shift in (1, 2, -1))


def fetch(piece_refs, held, sems):
    copies = [
        pltpu.make_async_copy(piece, held.at[index // 4, index % 4], sems.at[index])
        for index, piece in enumerate(piece_refs)
    ]
    for copy in copies:
        copy.start()
    for copy in copies:
        copy.wait()


def held_block(held, pos_ref, core_type, x_from, y_from, z_from):
    x_back = (pos_ref[0] - x_from) & 3
    y_back = (pos_ref[1] - y_from) & 3
    z_back = (pos_ref[2] - z_from) & 3
    who = pos_ref[3] ^ core_type
    if core_type == 0:
        block = held[who, y_back, x_back, z_back]
    else:
        block = held[who, x_back, y_back, z_back]
    return block.astype(jnp.float32)


def project_kernel(pos_ref, *refs):
    states, piece_refs, outs = refs[0], refs[1:9], refs[9:13]
    held, weight, by_shift, sems = refs[13:]
    fetch(piece_refs, held, sems)

    def place(index, carry):
        d, z_from, xl = index // 8, (index // 2) & 3, index & 1
        x_from, y_from = (d // 4) * 2 + xl, d & 3
        pair = jnp.concatenate(
            [held_block(held, pos_ref, ct, x_from, y_from, z_from) for ct in range(2)], axis=0
        )
        weight[pl.ds(pl.multiple_of(index * 80, 80), 80), :] = pair.astype(jnp.bfloat16)
        return carry

    lax.fori_loop(0, 64, place, 0)
    z = pos_ref[2]
    for half in range(2):
        rows = pl.ds(half * 2 * ROWS, 2 * ROWS)
        parts = [states[block, rows, :].astype(jnp.float32) for block in range(4)]
        total = sum(jnp.sum(part * part, axis=-1, keepdims=True) for part in parts)
        factor = lax.rsqrt(total / D + norm_epsilon)
        result = None
        for block, part in enumerate(parts):
            term = jnp.dot(
                (part * factor).astype(jnp.bfloat16),
                weight[block * OUT_COLS : (block + 1) * OUT_COLS, :],
                preferred_element_type=jnp.float32,
            )
            result = term if result is None else result + term
        result = result.astype(jnp.bfloat16)
        for inner in range(2):
            by_shift[(2 * half + inner - z) & 3] = result[inner * ROWS : (inner + 1) * ROWS]
    for shift in range(4):
        outs[shift][...] = by_shift[shift]


def order_kernel(halves_ref, weight, held, sem):
    copy = pltpu.make_async_copy(halves_ref, held, sem)
    copy.start()
    copy.wait()

    def place(index, carry):
        d, z_from = index // 4, index & 3
        for half in range(2):
            pair = jnp.concatenate(
                [held[d // 4, d & 3, xl, half, z_from].astype(jnp.float32) for xl in range(2)],
                axis=0,
            )
            weight[
                pl.ds(pl.multiple_of(index * 80, 80), 80),
                half * OUT_COLS // 2 : (half + 1) * OUT_COLS // 2,
            ] = pair.astype(jnp.bfloat16)
        return carry

    lax.fori_loop(0, 32, place, 0)


def output_kernel(pos_ref, *refs):
    lows, highs, states, weight, out_ref = refs[:4], refs[4:8], refs[8], refs[9], refs[10]
    z = pos_ref[2]
    for back in range(4):
        owner = (z - back) & 3
        part = jnp.concatenate([lows[back][...], highs[back][...]], axis=0)
        result = jnp.dot(part, weight[...], preferred_element_type=jnp.float32)
        rows = pl.ds(pl.multiple_of(owner * ROWS, ROWS), ROWS)
        result = (states[rows, :].astype(jnp.float32) + result).astype(jnp.bfloat16)
        for block in range(4):
            out_ref[block, owner] = result[:, block * FEATURES : (block + 1) * FEATURES]


SMEM_SPEC = pl.BlockSpec(memory_space=pltpu.SMEM)
VMEM_SPEC = pl.BlockSpec(memory_space=pltpu.VMEM)
ANY_SPEC = pl.BlockSpec(memory_space=pl.ANY)


def bf16(*shape):
    return jax.ShapeDtypeStruct(shape, jnp.bfloat16)


def params(mebibytes):
    return pltpu.CompilerParams(vmem_limit_bytes=mebibytes * 1024 * 1024)


def cost(flops, size):
    return pl.CostEstimate(flops=flops, bytes_accessed=size, transcendentals=0)


def project(position, states, pieces):
    return pl.pallas_call(
        project_kernel,
        out_shape=[bf16(ROWS, QKV_COLS)] * 4,
        in_specs=[SMEM_SPEC, VMEM_SPEC] + [ANY_SPEC] * 8,
        out_specs=[VMEM_SPEC] * 4,
        scratch_shapes=[
            pltpu.VMEM((2, 4, 4, 4, 40, QKV_COLS), jnp.bfloat16),
            pltpu.VMEM((D, QKV_COLS), jnp.bfloat16),
            pltpu.VMEM((4, ROWS, QKV_COLS), jnp.bfloat16),
            pltpu.SemaphoreType.DMA((8,)),
        ],
        compiler_params=params(40),
        cost_estimate=cost(8 * ROWS * D * QKV_COLS, 20000000),
    )(position, states, *pieces)


def order(halves):
    return pl.pallas_call(
        order_kernel,
        out_shape=bf16(ATT, OUT_COLS),
        in_specs=[ANY_SPEC],
        out_specs=VMEM_SPEC,
        scratch_shapes=[
            pltpu.VMEM(halves.shape, jnp.bfloat16),
            pltpu.SemaphoreType.DMA(()),
        ],
        compiler_params=params(24),
        cost_estimate=cost(0, 14000000),
    )(halves)


def project_out(position, lows, highs, states, weight):
    return pl.pallas_call(
        output_kernel,
        out_shape=bf16(4, 4, ROWS, FEATURES),
        in_specs=[SMEM_SPEC] + [VMEM_SPEC] * 10,
        out_specs=VMEM_SPEC,
        compiler_params=params(24),
        cost_estimate=cost(8 * ROWS * ATT * OUT_COLS, 12000000),
    )(position, *lows, *highs, states, weight)


def stack_kernel(*refs):
    for index in range(4):
        refs[5][index] = refs[index][:, :QKV_COLS]
        refs[6][index] = refs[index][:, QKV_COLS:]


def stack_blocks(blocks, states):
    return pl.pallas_call(
        stack_kernel,
        out_shape=[
            bf16(4, 40, QKV_COLS),
            bf16(4, 40, OUT_COLS // 2),
            jax.ShapeDtypeStruct(states.shape, states.dtype),
        ],
        in_specs=[VMEM_SPEC] * 4 + [ANY_SPEC],
        out_specs=[VMEM_SPEC] * 2 + [ANY_SPEC],
        input_output_aliases={4: 2},
    )(*blocks, states)


def halves_kernel(pos_ref, block_ref, *refs):
    c = pos_ref[3]
    for index in range(4):
        from_block = block_ref[(pos_ref[2] - index) & 3].astype(jnp.float32)
        low, high = from_block[:20], from_block[20:]
        refs[-2][index] = jnp.where(c == 0, low, high).astype(jnp.bfloat16)
        refs[-1][index] = jnp.where(c == 0, high, low).astype(jnp.bfloat16)


def halves_of(position, block, *after):
    return pl.pallas_call(
        halves_kernel,
        out_shape=[bf16(4, 20, OUT_COLS // 2)] * 2,
        in_specs=[SMEM_SPEC, VMEM_SPEC] + [ANY_SPEC] * len(after),
        out_specs=[VMEM_SPEC] * 2,
    )(position, block, *after)


def rotate(heads_in, cosine, sine_part):
    half_dim = HEAD_DIM // 2
    widened = heads_in.astype(jnp.float32)
    front_half = widened[..., :half_dim]
    back_half = widened[..., half_dim:]
    return jnp.concatenate(
        [front_half * cosine - back_half * sine_part, back_half * cosine + front_half * sine_part],
        axis=-1,
    ).astype(jnp.bfloat16)


def attend(projected, key_cache, value_cache, lengths):
    half_dim = HEAD_DIM // 2
    frequencies = rope_base ** (-2.0 * jnp.arange(half_dim, dtype=jnp.float32) / HEAD_DIM)
    positions = lengths[None, :] + jnp.arange(STEPS, dtype=jnp.int32)[:, None]
    angles = positions.astype(jnp.float32)[:, :, None] * frequencies
    cosine, sine_part = jnp.cos(angles)[:, :, None, :], jnp.sin(angles)[:, :, None, :]
    heads = projected.reshape(STEPS, PROMPT_DEV, HEADS + 2 * KV_HEADS, HEAD_DIM)
    rotated = rotate(heads[:, :, : HEADS + KV_HEADS], cosine, sine_part)
    queries = rotated[:, :, :HEADS].reshape(STEPS, PROMPT_DEV, KV_HEADS, GROUP, HEAD_DIM)
    queries = queries.transpose(1, 2, 0, 3, 4).reshape(
        PROMPT_DEV, KV_HEADS, STEPS * GROUP, HEAD_DIM
    )
    fresh_keys = rotated[:, :, HEADS:].transpose(1, 2, 0, 3)
    fresh_values = heads[:, :, HEADS + KV_HEADS :].transpose(1, 2, 0, 3)
    score_scale = HEAD_DIM ** (-0.5)
    cache_scores = (
        jnp.einsum("pkgd,pkld->pkgl", queries, key_cache, preferred_element_type=jnp.float32)
        * score_scale
    )
    fresh_scores = (
        jnp.einsum("pkgd,pksd->pkgs", queries, fresh_keys, preferred_element_type=jnp.float32)
        * score_scale
    )
    cache_mask = (jnp.arange(CACHE)[None, :] < lengths[:, None])[:, None, None, :]
    row_step = jnp.arange(STEPS * GROUP) // GROUP
    fresh_mask = (jnp.arange(STEPS)[None, :] <= row_step[:, None])[None, None]
    cache_scores = jnp.where(cache_mask, cache_scores, -1e30)
    fresh_scores = jnp.where(fresh_mask, fresh_scores, -1e30)
    largest = jnp.maximum(
        jnp.max(cache_scores, axis=-1, keepdims=True), jnp.max(fresh_scores, axis=-1, keepdims=True)
    )
    cache_exp = jnp.exp(cache_scores - largest)
    fresh_exp = jnp.exp(fresh_scores - largest)
    denominator = jnp.sum(cache_exp, axis=-1, keepdims=True) + jnp.sum(
        fresh_exp, axis=-1, keepdims=True
    )
    cache_weights = (cache_exp / denominator).astype(jnp.bfloat16)
    fresh_weights = (fresh_exp / denominator).astype(jnp.bfloat16)
    result = jnp.einsum(
        "pkgl,pkld->pkgd", cache_weights, value_cache, preferred_element_type=jnp.float32
    )
    result = result + jnp.einsum(
        "pkgs,pksd->pkgd", fresh_weights, fresh_values, preferred_element_type=jnp.float32
    )
    result = result.reshape(PROMPT_DEV, KV_HEADS, STEPS, GROUP, HEAD_DIM).transpose(2, 0, 1, 3, 4)
    return result.reshape(ROWS, ATT).astype(jnp.bfloat16)


def on_device(
    qkv_weight,
    out_weight,
    qkv_grad,
    out_grad,
    qkv_moment,
    out_moment,
    qkv_second,
    out_second,
    step_states,
    key_cache,
    value_cache,
    prompt_lengths,
):
    xh, y, z, xl, c = (lax.axis_index(axis) for axis in AXES)
    place = xl * 2 + c
    position = jnp.stack([xh * 2 + xl, y, z, c]).astype(jnp.int32)

    def trade(block_to):
        came = [block_to(place)]
        for other in range(1, 4):
            came.append(
                lax.ppermute(
                    block_to(place ^ other), ("xl", "c"), [(i, i ^ other) for i in range(4)]
                )
            )
        return [lax.select_n(place, *[came[i ^ j] for j in range(4)]) for i in range(4)]

    qkv_updated, qkv_moment_next, qkv_second_next = adam_update(
        qkv_weight, qkv_grad, qkv_moment, qkv_second
    )
    out_updated, out_moment_next, out_second_next = adam_update(
        out_weight, out_grad, out_moment, out_second
    )

    by_place = step_states.reshape(STEPS, 4, 4, PROMPT_DEV, FEATURES)
    by_place = by_place.transpose(2, 1, 0, 3, 4).reshape(4, 4 * ROWS, FEATURES)
    came = trade(lambda i: lax.dynamic_index_in_dim(by_place, i, 0, keepdims=False))
    own_states = jnp.concatenate(came, axis=-1)

    by_z = jnp.concatenate(
        [
            qkv_updated.reshape(40, 4, QKV_COLS).transpose(1, 0, 2),
            out_updated.reshape(20, 4, 2, OUT_COLS // 2)
            .transpose(1, 2, 0, 3)
            .reshape(4, 40, OUT_COLS // 2),
        ],
        axis=-1,
    )
    blocks = [lax.dynamic_index_in_dim(by_z, z, 0, keepdims=False)] + [
        z_permute(lax.dynamic_index_in_dim(by_z, (z + shift) & 3, 0, keepdims=False), shift)
        for shift in range(1, 4)
    ]
    qkv_block, out_block, own_states = stack_blocks(blocks, own_states)
    all_states = lax.all_gather(own_states, "z")
    qkv_pieces = plane_gather(qkv_block)
    qkv_pieces = qkv_pieces + tuple(core_permute(piece) for piece in qkv_pieces)
    projected = project(position, all_states, qkv_pieces)

    own_half, sent_half = halves_of(position, out_block, *qkv_pieces[1:4])
    other_half = core_permute(sent_half)
    both = jnp.where(
        c == 0,
        jnp.concatenate([own_half, other_half], axis=1),
        jnp.concatenate([other_half, own_half], axis=1),
    )
    gathered = lax.all_gather(both, ("xh", "y", "xl", "c"))
    out_columns = order(gathered.reshape(2, 4, 2, 2, 4, 40, OUT_COLS // 2))

    columns = [projected[0]] + [z_permute(projected[shift], shift) for shift in range(1, 4)]
    own_rows = jnp.concatenate(
        [lax.select_n(z, *[columns[(j - i) % 4] for j in range(4)]) for i in range(4)], axis=-1
    )
    attended = attend(own_rows, key_cache, value_cache, prompt_lengths)
    low_attended, high_attended = attended[: ROWS // 2], attended[ROWS // 2 :]
    low_ring, high_ring = z_ring(low_attended, high_attended)
    blocks = project_out(
        position,
        (low_attended,) + low_ring,
        (high_attended,) + high_ring,
        own_states,
        out_columns,
    )
    came = trade(lambda i: lax.dynamic_index_in_dim(blocks, i, 0, keepdims=False))
    outputs = jnp.stack(
        [block.reshape(4, STEPS, PROMPT_DEV, FEATURES) for block in came], axis=1
    )
    outputs = outputs.transpose(2, 0, 1, 3, 4).reshape(STEPS, 16 * PROMPT_DEV, FEATURES)
    return (
        qkv_updated,
        out_updated,
        qkv_moment_next,
        out_moment_next,
        qkv_second_next,
        out_second_next,
        outputs,
    )


def solution(mesh):
    fine = Mesh(mesh.devices.reshape(SIZES), AXES)
    rows = P(AXES, None)
    caches = P(AXES, None, None, None)
    states = P(None, ("xh", "y"), ("z", "xl", "c"))
    return jax.shard_map(
        on_device,
        mesh=fine,
        in_specs=(rows,) * 8 + (states, caches, caches, P(AXES)),
        out_specs=(rows,) * 6 + (states,),
        check_vma=False,
    )
```

profile of v0, /device:TPU:1, one launch (start us, length us, event | category | flops | bytes accessed | tf_op | source)
XLA Modules:
  0.0 184.0 jit_solution(3196517650919528855)
XLA Ops:
  7.2 1.7 copy.62
  9.2 1.5 collective-permute-start.3
  10.7 1.3 collective-permute-start.5
  12.3 2.5 %fusion.21 = (bf16[20,5120]{1,0:T(8,128)(2,1)S(1)}, f32[20,5120]{1,0:T(8,128)}, f32[20,5120]{1,0:T(8,128)}) fusion(bf16[20,5120]{1,0:T(8,128)(2,1)} %param.13, bf16[20,5120]{1,0:T(8,128)(2,1)} %param.15, f32[20,5120]{1,0:T(8,128)S(1)} %copy-done.12, f32[20,5120]{1,0:T(8,128)S(1)} %copy-done.13), kind=kLoop, calls=%fused_computation.50 | loop fusion | flops 1843200 | bytes 2252800 | tf_op jit(solution)/shard_map/convert_element_type | solution.py:49
  14.8 1.5 fusion.12
  16.6 0.8 fusion.34
  17.4 1.8 collective-permute-start
  19.1 3.3 %collective-permute-start.1 = (bf16[40,1536]{1,0:T(8,128)(2,1)}, bf16[40,1536]{1,0:T(8,128)(2,1)}, u32[]{:S(2)}, u32[]{:S(2)}) collective-permute-start(bf16[40,1536]{1,0:T(8,128)(2,1)} %get-tuple-element.77), channel_id=1, source_target_pairs={{0,8},{4,12},{8,0},{12,4},{1,9},{5,13},{9,1},{13,5},{2,10},{6,14},... | collective-permute-start | bytes 368648 | tf_op jit(solution)/shard_map/ppermute | solution.py:75
  22.4 0.7 collective-permute-start.2
  23.2 2.4 %collective-permute-done.4 = bf16[384,320]{1,0:T(8,128)(2,1)} collective-permute-done((bf16[384,320]{1,0:T(8,128)(2,1)S(1)}, bf16[384,320]{1,0:T(8,128)(2,1)}, u32[]{:S(2)}, u32[]{:S(2)}) %collective-permute-start.4) | collective-permute-done | bytes 245792 | tf_op jit(solution)/shard_map/ppermute | solution.py:373
  25.6 1.3 fusion.31
  26.9 1.9 %concatenate.38.refs_4_ = bf16[384,1280]{1,0:T(8,128)(2,1)} concatenate(bf16[384,320]{1,0:T(8,128)(2,1)S(1)} %get-tuple-element.59, bf16[384,320]{1,0:T(8,128)(2,1)S(1)} %get-tuple-element.58, bf16[384,320]{1,0:T(8,128)(2,1)S(1)} %get-tuple-element.57, bf16[384,320]{1,0:T(8,128)(2,1)S(1)} %get-tuple-element.56), dimensions={1} | concatenate | bytes 1966080 | tf_op jit(solution)/shard_map/concatenate | solution.py:389
  28.9 0.6 copy-done.17
  29.5 1.9 %shard_map.171 = (bf16[4,40,896]{2,1,0:T(8,128)(2,1)}, bf16[4,40,640]{2,1,0:T(8,128)(2,1)}, bf16[384,1280]{1,0:T(8,128)(2,1)}) custom-call(bf16[40,1536]{1,0:T(8,128)(2,1)} %get-tuple-element.75.refs_0_, bf16[40,1536]{1,0:T(8,128)(2,1)} %copy-done.17, bf16[40,1536]{1,0:T(8,128)(2,1)} %collective-permute-done.1.refs_2_, ...), custom_call_target="tpu_custom_call", output_to_operand_aliasing={{2}: (4, {})} | custom-call | tf_op jit(solution)/shard_map/pallas_call | solution.py:261
  31.5 2.9 %collective-permute-start.8 = (bf16[4,40,896]{2,1,0:T(8,128)(2,1)}, bf16[4,40,896]{2,1,0:T(8,128)(2,1)S(1)}, u32[]{:S(2)}, u32[]{:S(2)}) collective-permute-start(bf16[4,40,896]{2,1,0:T(8,128)(2,1)} %get-tuple-element.17), channel_id=1, source_target_pairs={{0,66},{1,49},{4,70},{5,53},{8,74},{9,57},{12,78},{13,61},{16,82},... | collective-permute-start | bytes 860168 | tf_op jit(solution)/shard_map/ppermute | solution.py:71
  34.7 0.7 collective-permute-start.6
  35.4 5.9 %collective-permute-done.8 = bf16[4,40,896]{2,1,0:T(8,128)(2,1)S(1)} collective-permute-done((bf16[4,40,896]{2,1,0:T(8,128)(2,1)}, bf16[4,40,896]{2,1,0:T(8,128)(2,1)S(1)}, u32[]{:S(2)}, u32[]{:S(2)}) %collective-permute-start.8) | collective-permute-done | bytes 286752 | tf_op jit(solution)/shard_map/ppermute | solution.py:71
  41.4 0.6 collective-permute-done.7
  41.9 3.0 %collective-permute-done.6 = bf16[4,40,896]{2,1,0:T(8,128)(2,1)S(1)} collective-permute-done((bf16[4,40,896]{2,1,0:T(8,128)(2,1)}, bf16[4,40,896]{2,1,0:T(8,128)(2,1)S(1)}, u32[]{:S(2)}, u32[]{:S(2)}) %collective-permute-start.6) | collective-permute-done | bytes 286752 | tf_op jit(solution)/shard_map/ppermute | solution.py:71
  45.1 1.0 collective-permute-start.9
  46.1 2.5 %collective-permute-start.10 = (bf16[4,4,40,896]{3,2,1,0:T(8,128)(2,1)S(1)}, bf16[4,4,40,896]{3,2,1,0:T(8,128)(2,1)S(1)}, u32[]{:S(2)}, u32[]{:S(2)}) collective-permute-start(bf16[4,4,40,896]{3,2,1,0:T(8,128)(2,1)S(1)} %pad_maximum_fusion.refs_1_), channel_id=1, source_target_pairs={{0,32},{1,65},{4,36},{5,69},{8,40},{9,73},{12,44},{13,77},{16,48},... | collective-permute-start | bytes 3440648 | tf_op jit(solution)/shard_map/ppermute | solution.py:71
  48.6 1.2 collective-permute-start.11
  49.7 0.6 pad_add_fusion.pos_ref
  50.3 11.2 %collective-permute-done.9.refs_2_.refs_0_ = bf16[4,4,40,896]{3,2,1,0:T(8,128)(2,1)S(1)} collective-permute-done((bf16[4,4,40,896]{3,2,1,0:T(8,128)(2,1)S(1)}, bf16[4,4,40,896]{3,2,1,0:T(8,128)(2,1)S(1)}, u32[]{:S(2)}, u32[]{:S(2)}) %collective-permute-start.9) | collective-permute-done | bytes 1146912 | tf_op jit(solution)/shard_map/ppermute | solution.py:71
  61.5 12.9 %collective-permute-done.10.refs_3_.refs_1_ = bf16[4,4,40,896]{3,2,1,0:T(8,128)(2,1)S(1)} collective-permute-done((bf16[4,4,40,896]{3,2,1,0:T(8,128)(2,1)S(1)}, bf16[4,4,40,896]{3,2,1,0:T(8,128)(2,1)S(1)}, u32[]{:S(2)}, u32[]{:S(2)}) %collective-permute-start.10) | collective-permute-done | bytes 1146912 | tf_op jit(solution)/shard_map/ppermute | solution.py:71
  74.4 1.0 copy-done.4
  75.4 1.7 shard_map.173
  77.1 3.2 %collective-permute-start.25 = (bf16[4,20,640]{2,1,0:T(8,128)(2,1)}, bf16[4,20,640]{2,1,0:T(8,128)(2,1)S(1)}, u32[]{:S(2)}, u32[]{:S(2)}) collective-permute-start(bf16[4,20,640]{2,1,0:T(8,128)(2,1)} %get-tuple-element.24), channel_id=1, source_target_pairs={{0,1},{1,0},{2,3},{3,2},{4,5},{5,4},{6,7},{7,6},{8,9},{9,8},{10,11... | collective-permute-start | bytes 307208 | tf_op jit(solution)/shard_map/ppermute | solution.py:79
  80.4 1.2 collective-permute-done.25
  81.6 1.8 maximum_select_fusion
  84.4 0.5 and_select_fusion
  85.6 0.8 collective-permute-done.12.refs_5_
  86.3 3.4 %collective-permute-done.13.refs_6_ = bf16[4,4,40,896]{3,2,1,0:T(8,128)(2,1)S(1)} collective-permute-done((bf16[4,4,40,896]{3,2,1,0:T(8,128)(2,1)}, bf16[4,4,40,896]{3,2,1,0:T(8,128)(2,1)S(1)}, u32[]{:S(2)}, u32[]{:S(2)}) %collective-permute-start.13) | collective-permute-done | bytes 1146912 | tf_op jit(solution)/shard_map/ppermute | solution.py:79
  89.8 1.6 collective-permute-done.15.refs_8_
  91.5 1.3 copy-done.3
  92.8 1.3 copy-done.5
  94.0 2.2 %copy-done.6 = bf16[1536,1280]{1,0:T(8,128)(2,1)S(1)} copy-done((bf16[1536,1280]{1,0:T(8,128)(2,1)S(1)}, bf16[1536,1280]{1,0:T(8,128)(2,1)}, u32[]{:S(2)}) %copy-start.6) | copy-done | bytes 3932184
  96.2 10.4 %shard_map.172 = (bf16[96,896]{1,0:T(8,128)(2,1)S(1)}, bf16[96,896]{1,0:T(8,128)(2,1)S(1)}, bf16[96,896]{1,0:T(8,128)(2,1)S(1)}, bf16[96,896]{1,0:T(8,128)(2,1)S(1)}) custom-call(s32[4]{0:T(128)S(1)} %copy-done.7, bf16[4,384,1280]{2,1,0:T(8,128)(2,1)S(1)} %bitcast.97, bf16[4,4,40,896]{3,2,1,0:T(8,128)(2,1)S(1)} %pad_maximum_fusion.refs_1_, ...), custom_call_target="tpu_custom_call" | custom-call | flops 3523215360 | bytes 20000000 | tf_op jit(solution)/shard_map/pallas_call | solution.py:212
  106.6 3.7 %collective-permute-start.17 = (bf16[96,896]{1,0:T(8,128)(2,1)S(1)}, bf16[96,896]{1,0:T(8,128)(2,1)S(1)}, u32[]{:S(2)}, u32[]{:S(2)}) collective-permute-start(bf16[96,896]{1,0:T(8,128)(2,1)S(1)} %get-tuple-element.20), channel_id=1, source_target_pairs={{0,8},{4,12},{8,0},{12,4},{1,9},{5,13},{9,1},{13,5},{2,10},{6,14},... | collective-permute-start | bytes 516104 | tf_op jit(solution)/shard_map/ppermute | solution.py:75
  110.7 1.1 collective-permute-start.16
  111.8 3.0 %collective-permute-done.17 = bf16[96,896]{1,0:T(8,128)(2,1)S(1)} collective-permute-done((bf16[96,896]{1,0:T(8,128)(2,1)S(1)}, bf16[96,896]{1,0:T(8,128)(2,1)S(1)}, u32[]{:S(2)}, u32[]{:S(2)}) %collective-permute-start.17) | collective-permute-done | bytes 172064 | tf_op jit(solution)/shard_map/ppermute | solution.py:75
  114.8 4.2 %collective-permute-done.18 = bf16[96,896]{1,0:T(8,128)(2,1)S(1)} collective-permute-done((bf16[96,896]{1,0:T(8,128)(2,1)S(1)}, bf16[96,896]{1,0:T(8,128)(2,1)S(1)}, u32[]{:S(2)}, u32[]{:S(2)}) %collective-permute-start.18) | collective-permute-done | bytes 172064 | tf_op jit(solution)/shard_map/ppermute | solution.py:75
  120.1 0.9 add_convert_fusion
  121.0 0.7 fusion.18
  121.9 0.5 fusion.54
  122.4 7.0 %fusion = (f32[24,4,20]{2,1,0:T(4,128)S(1)}, f32[24,4,20,320]{3,2,1,0:T(8,128)S(1)}) fusion(pred[24,320]{1,0:T(8,128)(4,1)S(1)} %iota_compare_fusion, bf16[24,4,320,128]{3,2,1,0:T(8,128)(2,1)} %param.21, bf16[24,4,20,128]{3,0,2,1:T(8,128)(2,1)S(1)} %bitcast.99), kind=kOutput, calls=%fused_computation.3 | convolution fusion | flops 159127680 | bytes 10828800 | tf_op jit(solution)/shard_map/pkgd,pkld->pkgl/dot_general | solution.py:319
  129.7 1.7 fusion.1
  131.4 1.9 %fusion.2 = f32[24,4,20,128]{3,2,1,0:T(8,128)S(1)} fusion(bf16[24,4,320,128]{3,2,1,0:T(8,128)(2,1)S(1)} %bitcast.120, f32[24,4,20,320]{3,2,1,0:T(8,128)S(1)} %get-tuple-element.81, f32[24,4,20]{2,1,0:T(4,128)S(1)} %add.139, f32[24,4,20]{2,1,0:T(4,128)S(1)} %max.8, pred[24,320]{1,0:T(8,128)(4,1)S(1)} %iota_compare_fusion), kind=kOutput, calls=%fused_computation.5 | convolution fusion | flops 160358400 | bytes 11328000 | tf_op jit(solution)/shard_map/pkgl,pkld->pkgd/dot_general | solution.py:341
  133.4 0.6 fusion.8
  134.6 0.9 collective-permute-start.19
  135.8 2.1 %collective-permute-start.23 = (bf16[48,2560]{1,0:T(8,128)(2,1)S(1)}, bf16[48,2560]{1,0:T(8,128)(2,1)S(1)}, u32[]{:S(2)}, u32[]{:S(2)}) collective-permute-start(bf16[48,2560]{1,0:T(8,128)(2,1)S(1)} %slice.39.refs_4_), channel_id=1, source_target_pairs={{0,12},{4,0},{8,4},{12,8},{1,13},{5,1},{9,5},{13,9},{2,14},{6,2},{... | collective-permute-start | bytes 737288 | tf_op jit(solution)/shard_map/ppermute | solution.py:75
  137.9 1.4 collective-permute-start.21
  139.4 3.1 %collective-permute-done.19.refs_1_ = bf16[48,2560]{1,0:T(8,128)(2,1)S(1)} collective-permute-done((bf16[48,2560]{1,0:T(8,128)(2,1)S(1)}, bf16[48,2560]{1,0:T(8,128)(2,1)S(1)}, u32[]{:S(2)}, u32[]{:S(2)}) %collective-permute-start.19) | collective-permute-done | bytes 245792 | tf_op jit(solution)/shard_map/ppermute | solution.py:75
  142.5 2.8 %collective-permute-start.24 = (bf16[48,2560]{1,0:T(8,128)(2,1)S(1)}, bf16[48,2560]{1,0:T(8,128)(2,1)S(1)}, u32[]{:S(2)}, u32[]{:S(2)}) collective-permute-start(bf16[48,2560]{1,0:T(8,128)(2,1)S(1)} %collective-permute-done.23.refs_7_), channel_id=1, source_target_pairs={{0,12},{4,0},{8,4},{12,8},{1,13},{5,1},{9,5},{13,9},{2,14},{6,2},{... | collective-permute-start | bytes 737288 | tf_op jit(solution)/shard_map/ppermute | solution.py:75
  145.3 1.0 all-gather.4.cloned.1.call-done
  146.3 2.9 %copy-done.1 = bf16[32,4,40,640]{3,2,1,0:T(8,128)(2,1)S(1)} copy-done((bf16[32,4,40,640]{3,2,1,0:T(8,128)(2,1)S(1)}, bf16[32,4,40,640]{3,2,1,0:T(8,128)(2,1)}, u32[]{:S(2)}) %copy-start.1) | copy-done | bytes 6553624
  149.2 1.5 shard_map.174.refs_9_
  150.7 2.6 %collective-permute-done.20.refs_2_ = bf16[48,2560]{1,0:T(8,128)(2,1)S(1)} collective-permute-done((bf16[48,2560]{1,0:T(8,128)(2,1)S(1)}, bf16[48,2560]{1,0:T(8,128)(2,1)S(1)}, u32[]{:S(2)}, u32[]{:S(2)}) %collective-permute-start.20) | collective-permute-done | bytes 245792 | tf_op jit(solution)/shard_map/ppermute | solution.py:75
  153.3 4.9 %shard_map.175 = bf16[4,4,96,320]{3,2,1,0:T(8,128)(2,1)S(1)} custom-call(s32[4]{0:T(128)S(1)} %copy-done.7, bf16[48,2560]{1,0:T(8,128)(2,1)S(1)} %slice.37.refs_0_, bf16[48,2560]{1,0:T(8,128)(2,1)S(1)} %collective-permute-done.19.refs_1_, bf16[48,2560]{1,0:T(8,128)(2,1)S(1)} %collective-permute-done.20.refs_2_, ...), custom_call_target="tpu_custom_call" | custom-call | flops 2516582400 | bytes 12000000 | tf_op jit(solution)/shard_map/pallas_call | solution.py:244
  158.3 1.8 collective-permute-start.26
  160.1 1.7 collective-permute-start.28
  161.8 6.8 %collective-permute-done.27 = bf16[4,96,320]{2,1,0:T(8,128)(2,1)S(1)} collective-permute-done((bf16[4,96,320]{2,1,0:T(8,128)(2,1)S(1)}, bf16[4,96,320]{2,1,0:T(8,128)(2,1)S(1)}, u32[]{:S(2)}, u32[]{:S(2)}) %collective-permute-start.27) | collective-permute-done | bytes 245792 | tf_op jit(solution)/shard_map/ppermute | solution.py:373
  168.6 6.5 %collective-permute-done.28 = bf16[4,96,320]{2,1,0:T(8,128)(2,1)S(1)} collective-permute-done((bf16[4,96,320]{2,1,0:T(8,128)(2,1)S(1)}, bf16[4,96,320]{2,1,0:T(8,128)(2,1)S(1)}, u32[]{:S(2)}, u32[]{:S(2)}) %collective-permute-start.28) | collective-permute-done | bytes 245792 | tf_op jit(solution)/shard_map/ppermute | solution.py:373
  175.8 1.4 copy.73
  (101 shorter events, 6.9 us)
Async XLA Ops:
  7.2 84.3 %all-gather.6.cloned.1.call-start = ((), (), s32[]{:S(2)}) async-start(), calls=%async_computation.1 | async-start | bytes 4915200 | tf_op jit(solution)/shard_map/all_gather | solution.py:405
  9.1 3.2 %copy-start.12 = (f32[20,5120]{1,0:T(8,128)S(1)}, f32[20,5120]{1,0:T(8,128)}, u32[]{:S(2)}) copy-start(f32[20,5120]{1,0:T(8,128)} %param.17) | copy-start | bytes 1228804
  9.1 3.2 %copy-start.13 = (f32[20,5120]{1,0:T(8,128)S(1)}, f32[20,5120]{1,0:T(8,128)}, u32[]{:S(2)}) copy-start(f32[20,5120]{1,0:T(8,128)} %param.19) | copy-start | bytes 1228804
  9.2 13.2 %collective-permute-start.3 = (bf16[384,320]{1,0:T(8,128)(2,1)S(1)}, bf16[384,320]{1,0:T(8,128)(2,1)}, u32[]{:S(2)}, u32[]{:S(2)}) collective-permute-start(bf16[384,320]{1,0:T(8,128)(2,1)S(1)} %get-tuple-element.67), channel_id=1, source_target_pairs={{0,1},{1,0},{2,3},{3,2},{4,5},{5,4},{6,7},{7,6},{8,9},{9,8},{10,11... | collective-permute-start | bytes 737288 | tf_op jit(solution)/shard_map/ppermute | solution.py:373
  10.7 12.4 %collective-permute-start.5 = (bf16[384,320]{1,0:T(8,128)(2,1)S(1)}, bf16[384,320]{1,0:T(8,128)(2,1)}, u32[]{:S(2)}, u32[]{:S(2)}) collective-permute-start(bf16[384,320]{1,0:T(8,128)(2,1)S(1)} %get-tuple-element.65), channel_id=1, source_target_pairs={{0,3},{1,2},{2,1},{3,0},{4,7},{5,6},{6,5},{7,4},{8,11},{9,10},{10,... | collective-permute-start | bytes 737288 | tf_op jit(solution)/shard_map/ppermute | solution.py:373
  12.0 2.8 %copy-start.10 = (f32[40,3584]{1,0:T(8,128)S(1)}, f32[40,3584]{1,0:T(8,128)}, u32[]{:S(2)}) copy-start(f32[40,3584]{1,0:T(8,128)} %param.16) | copy-start | bytes 1720324
  12.0 2.8 %copy-start.11 = (f32[40,3584]{1,0:T(8,128)S(1)}, f32[40,3584]{1,0:T(8,128)}, u32[]{:S(2)}) copy-start(f32[40,3584]{1,0:T(8,128)} %param.18) | copy-start | bytes 1720324
  12.0 2.8 %copy-start.14 = (bf16[40,3584]{1,0:T(8,128)(2,1)S(1)}, bf16[40,3584]{1,0:T(8,128)(2,1)}, u32[]{:S(2)}) copy-start(bf16[40,3584]{1,0:T(8,128)(2,1)} %param.12) | copy-start | bytes 860164
  12.0 2.8 %copy-start.15 = (bf16[40,3584]{1,0:T(8,128)(2,1)S(1)}, bf16[40,3584]{1,0:T(8,128)(2,1)}, u32[]{:S(2)}) copy-start(bf16[40,3584]{1,0:T(8,128)(2,1)} %param.14) | copy-start | bytes 860164
  12.0 13.6 %collective-permute-start.4 = (bf16[384,320]{1,0:T(8,128)(2,1)S(1)}, bf16[384,320]{1,0:T(8,128)(2,1)}, u32[]{:S(2)}, u32[]{:S(2)}) collective-permute-start(bf16[384,320]{1,0:T(8,128)(2,1)S(1)} %get-tuple-element.66), channel_id=1, source_target_pairs={{0,2},{1,3},{2,0},{3,1},{4,6},{5,7},{6,4},{7,5},{8,10},{9,11},{10,... | collective-permute-start | bytes 737288 | tf_op jit(solution)/shard_map/ppermute | solution.py:373
  14.8 1.6 copy-start.9
  16.3 1.0 copy-start.8
  17.4 11.5 %collective-permute-start = (bf16[40,1536]{1,0:T(8,128)(2,1)}, bf16[40,1536]{1,0:T(8,128)(2,1)S(1)}, u32[]{:S(2)}, u32[]{:S(2)}) collective-permute-start(bf16[40,1536]{1,0:T(8,128)(2,1)} %get-tuple-element.76), channel_id=1, source_target_pairs={{0,4},{4,8},{8,12},{12,0},{1,5},{5,9},{9,13},{13,1},{2,6},{6,10},{... | collective-permute-start | bytes 368648 | tf_op jit(solution)/shard_map/ppermute | solution.py:75
  19.1 9.7 %collective-permute-start.1 = (bf16[40,1536]{1,0:T(8,128)(2,1)}, bf16[40,1536]{1,0:T(8,128)(2,1)}, u32[]{:S(2)}, u32[]{:S(2)}) collective-permute-start(bf16[40,1536]{1,0:T(8,128)(2,1)} %get-tuple-element.77), channel_id=1, source_target_pairs={{0,8},{4,12},{8,0},{12,4},{1,9},{5,13},{9,1},{13,5},{2,10},{6,14},... | collective-permute-start | bytes 368648 | tf_op jit(solution)/shard_map/ppermute | solution.py:75
  22.4 6.4 %collective-permute-start.2 = (bf16[40,1536]{1,0:T(8,128)(2,1)S(1)}, bf16[40,1536]{1,0:T(8,128)(2,1)S(1)}, u32[]{:S(2)}, u32[]{:S(2)}) collective-permute-start(bf16[40,1536]{1,0:T(8,128)(2,1)S(1)} %get-tuple-element.74), channel_id=1, source_target_pairs={{0,12},{4,0},{8,4},{12,8},{1,13},{5,1},{9,5},{13,9},{2,14},{6,2},{... | collective-permute-start | bytes 368648 | tf_op jit(solution)/shard_map/ppermute | solution.py:75
  28.8 0.6 copy-start.17
  28.8 0.7 copy-start.18
  31.4 13.5 %copy-start.16 = (bf16[4,40,896]{2,1,0:T(8,128)(2,1)S(1)}, bf16[4,40,896]{2,1,0:T(8,128)(2,1)}, u32[]{:S(2)}) copy-start(bf16[4,40,896]{2,1,0:T(8,128)(2,1)} %get-tuple-element.17) | copy-start | bytes 860164
  31.5 114.8 %all-gather.4.cloned.1.call-start = ((), (), s32[]{:S(2)}) async-start(), calls=%async_computation | async-start | bytes 6758400 | tf_op jit(solution)/shard_map/all_gather | solution.py:417
  31.5 9.9 %collective-permute-start.8 = (bf16[4,40,896]{2,1,0:T(8,128)(2,1)}, bf16[4,40,896]{2,1,0:T(8,128)(2,1)S(1)}, u32[]{:S(2)}, u32[]{:S(2)}) collective-permute-start(bf16[4,40,896]{2,1,0:T(8,128)(2,1)} %get-tuple-element.17), channel_id=1, source_target_pairs={{0,66},{1,49},{4,70},{5,53},{8,74},{9,57},{12,78},{13,61},{16,82},... | collective-permute-start | bytes 860168 | tf_op jit(solution)/shard_map/ppermute | solution.py:71
  34.4 7.5 %collective-permute-start.7 = (bf16[4,40,896]{2,1,0:T(8,128)(2,1)}, bf16[4,40,896]{2,1,0:T(8,128)(2,1)S(1)}, u32[]{:S(2)}, u32[]{:S(2)}) collective-permute-start(bf16[4,40,896]{2,1,0:T(8,128)(2,1)} %get-tuple-element.17), channel_id=1, source_target_pairs={{0,64},{1,33},{4,68},{5,37},{8,72},{9,41},{12,76},{13,45},{16,80},... | collective-permute-start | bytes 860168 | tf_op jit(solution)/shard_map/ppermute | solution.py:71
  34.7 10.2 %collective-permute-start.6 = (bf16[4,40,896]{2,1,0:T(8,128)(2,1)}, bf16[4,40,896]{2,1,0:T(8,128)(2,1)S(1)}, u32[]{:S(2)}, u32[]{:S(2)}) collective-permute-start(bf16[4,40,896]{2,1,0:T(8,128)(2,1)} %get-tuple-element.17), channel_id=1, source_target_pairs={{0,2},{1,17},{4,6},{5,21},{8,10},{9,25},{12,14},{13,29},{16,18},{1... | collective-permute-start | bytes 860168 | tf_op jit(solution)/shard_map/ppermute | solution.py:71
  45.1 16.4 %collective-permute-start.9 = (bf16[4,4,40,896]{3,2,1,0:T(8,128)(2,1)S(1)}, bf16[4,4,40,896]{3,2,1,0:T(8,128)(2,1)S(1)}, u32[]{:S(2)}, u32[]{:S(2)}) collective-permute-start(bf16[4,4,40,896]{3,2,1,0:T(8,128)(2,1)S(1)} %pad_maximum_fusion.refs_1_), channel_id=1, source_target_pairs={{0,16},{1,3},{4,20},{5,7},{8,24},{9,11},{12,28},{13,15},{16,32},{1... | collective-permute-start | bytes 3440648 | tf_op jit(solution)/shard_map/ppermute | solution.py:71
  46.1 28.3 %collective-permute-start.10 = (bf16[4,4,40,896]{3,2,1,0:T(8,128)(2,1)S(1)}, bf16[4,4,40,896]{3,2,1,0:T(8,128)(2,1)S(1)}, u32[]{:S(2)}, u32[]{:S(2)}) collective-permute-start(bf16[4,4,40,896]{3,2,1,0:T(8,128)(2,1)S(1)} %pad_maximum_fusion.refs_1_), channel_id=1, source_target_pairs={{0,32},{1,65},{4,36},{5,69},{8,40},{9,73},{12,44},{13,77},{16,48},... | collective-permute-start | bytes 3440648 | tf_op jit(solution)/shard_map/ppermute | solution.py:71
  48.6 25.9 %collective-permute-start.11 = (bf16[4,4,40,896]{3,2,1,0:T(8,128)(2,1)S(1)}, bf16[4,4,40,896]{3,2,1,0:T(8,128)(2,1)}, u32[]{:S(2)}, u32[]{:S(2)}) collective-permute-start(bf16[4,4,40,896]{3,2,1,0:T(8,128)(2,1)S(1)} %pad_maximum_fusion.refs_1_), channel_id=1, source_target_pairs={{0,48},{1,67},{4,52},{5,71},{8,56},{9,75},{12,60},{13,79},{16,0},{... | collective-permute-start | bytes 3440648 | tf_op jit(solution)/shard_map/ppermute | solution.py:71
  61.5 12.9 %copy-start.2 = (bf16[4,4,40,896]{3,2,1,0:T(8,128)(2,1)}, bf16[4,4,40,896]{3,2,1,0:T(8,128)(2,1)S(1)}, u32[]{:S(2)}) copy-start(bf16[4,4,40,896]{3,2,1,0:T(8,128)(2,1)S(1)} %collective-permute-done.9.refs_2_.refs_0_) | copy-start | bytes 3440644
  74.4 1.0 copy-start.4
  75.4 9.6 %copy-start.19 = (s32[24]{0:T(128)S(1)}, s32[24]{0:T(128)}, u32[]{:S(2)}) copy-start(s32[24]{0:T(128)} %param.23) | copy-start | bytes 292
  75.4 16.1 %copy-start.7 = (s32[4]{0:T(128)S(1)}, s32[4]{0:T(128)}, u32[]{:S(2)}) copy-start(s32[4]{0:T(128)} %pad_add_fusion.pos_ref) | copy-start | bytes 52
  77.1 4.4 %collective-permute-start.25 = (bf16[4,20,640]{2,1,0:T(8,128)(2,1)}, bf16[4,20,640]{2,1,0:T(8,128)(2,1)S(1)}, u32[]{:S(2)}, u32[]{:S(2)}) collective-permute-start(bf16[4,20,640]{2,1,0:T(8,128)(2,1)} %get-tuple-element.24), channel_id=1, source_target_pairs={{0,1},{1,0},{2,3},{3,2},{4,5},{5,4},{6,7},{7,6},{8,9},{9,8},{10,11... | collective-permute-start | bytes 307208 | tf_op jit(solution)/shard_map/ppermute | solution.py:79
  83.3 3.0 %collective-permute-start.12 = (bf16[4,4,40,896]{3,2,1,0:T(8,128)(2,1)S(1)}, bf16[4,4,40,896]{3,2,1,0:T(8,128)(2,1)S(1)}, u32[]{:S(2)}, u32[]{:S(2)}) collective-permute-start(bf16[4,4,40,896]{3,2,1,0:T(8,128)(2,1)S(1)} %pad_maximum_fusion.refs_1_), channel_id=1, source_target_pairs={{0,1},{1,0},{2,3},{3,2},{4,5},{5,4},{6,7},{7,6},{8,9},{9,8},{10,11... | collective-permute-start | bytes 3440648 | tf_op jit(solution)/shard_map/ppermute | solution.py:79
  83.8 5.9 %collective-permute-start.13 = (bf16[4,4,40,896]{3,2,1,0:T(8,128)(2,1)}, bf16[4,4,40,896]{3,2,1,0:T(8,128)(2,1)S(1)}, u32[]{:S(2)}, u32[]{:S(2)}) collective-permute-start(bf16[4,4,40,896]{3,2,1,0:T(8,128)(2,1)} %copy-done.2), channel_id=1, source_target_pairs={{0,1},{1,0},{2,3},{3,2},{4,5},{5,4},{6,7},{7,6},{8,9},{9,8},{10,11... | collective-permute-start | bytes 3440648 | tf_op jit(solution)/shard_map/ppermute | solution.py:79
  83.9 5.9 %collective-permute-start.14 = (bf16[4,4,40,896]{3,2,1,0:T(8,128)(2,1)}, bf16[4,4,40,896]{3,2,1,0:T(8,128)(2,1)}, u32[]{:S(2)}, u32[]{:S(2)}) collective-permute-start(bf16[4,4,40,896]{3,2,1,0:T(8,128)(2,1)} %copy-done.4), channel_id=1, source_target_pairs={{0,1},{1,0},{2,3},{3,2},{4,5},{5,4},{6,7},{7,6},{8,9},{9,8},{10,11... | collective-permute-start | bytes 3440648 | tf_op jit(solution)/shard_map/ppermute | solution.py:79
  84.3 7.2 %collective-permute-start.15 = (bf16[4,4,40,896]{3,2,1,0:T(8,128)(2,1)}, bf16[4,4,40,896]{3,2,1,0:T(8,128)(2,1)}, u32[]{:S(2)}, u32[]{:S(2)}) collective-permute-start(bf16[4,4,40,896]{3,2,1,0:T(8,128)(2,1)} %collective-permute-done.11.refs_4_.refs_2_), channel_id=1, source_target_pairs={{0,1},{1,0},{2,3},{3,2},{4,5},{5,4},{6,7},{7,6},{8,9},{9,8},{10,11... | collective-permute-start | bytes 3440648 | tf_op jit(solution)/shard_map/ppermute | solution.py:79
  91.5 1.3 copy-start.3
  92.8 1.3 copy-start.5
  94.0 2.2 %copy-start.6 = (bf16[1536,1280]{1,0:T(8,128)(2,1)S(1)}, bf16[1536,1280]{1,0:T(8,128)(2,1)}, u32[]{:S(2)}) copy-start(bf16[1536,1280]{1,0:T(8,128)(2,1)} %all-gather.6.cloned.1.call-done) | copy-start | bytes 11796484
  96.2 15.6 %copy-start.20 = (s32[20]{0:T(128)S(1)}, s32[20]{0:T(128)}, u32[]{:S(2)}) copy-start(s32[20]{0:T(128)} %and_select_fusion) | copy-start | bytes 244
  106.6 8.1 %collective-permute-start.17 = (bf16[96,896]{1,0:T(8,128)(2,1)S(1)}, bf16[96,896]{1,0:T(8,128)(2,1)S(1)}, u32[]{:S(2)}, u32[]{:S(2)}) collective-permute-start(bf16[96,896]{1,0:T(8,128)(2,1)S(1)} %get-tuple-element.20), channel_id=1, source_target_pairs={{0,8},{4,12},{8,0},{12,4},{1,9},{5,13},{9,1},{13,5},{2,10},{6,14},... | collective-permute-start | bytes 516104 | tf_op jit(solution)/shard_map/ppermute | solution.py:75
  110.3 8.7 %collective-permute-start.18 = (bf16[96,896]{1,0:T(8,128)(2,1)S(1)}, bf16[96,896]{1,0:T(8,128)(2,1)S(1)}, u32[]{:S(2)}, u32[]{:S(2)}) collective-permute-start(bf16[96,896]{1,0:T(8,128)(2,1)S(1)} %get-tuple-element.21), channel_id=1, source_target_pairs={{0,12},{4,0},{8,4},{12,8},{1,13},{5,1},{9,5},{13,9},{2,14},{6,2},{... | collective-permute-start | bytes 516104 | tf_op jit(solution)/shard_map/ppermute | solution.py:75
  110.7 8.3 %collective-permute-start.16 = (bf16[96,896]{1,0:T(8,128)(2,1)S(1)}, bf16[96,896]{1,0:T(8,128)(2,1)S(1)}, u32[]{:S(2)}, u32[]{:S(2)}) collective-permute-start(bf16[96,896]{1,0:T(8,128)(2,1)S(1)} %get-tuple-element.19), channel_id=1, source_target_pairs={{0,4},{4,8},{8,12},{12,0},{1,5},{5,9},{9,13},{13,1},{2,6},{6,10},{... | collective-permute-start | bytes 516104 | tf_op jit(solution)/shard_map/ppermute | solution.py:75
  121.9 9.6 %slice-start = ((s8[7864320]{0:T(1024)(128)(4,1)}), s8[4194304]{0:T(1024)(128)(4,1)S(1)}, s32[]{:S(2)}) async-start(s8[7864320]{0:T(1024)(128)(4,1)} %bitcast.119), calls=%async_computation.2 | async-start | bytes 8388608
  122.4 9.0 %slice-start.1 = ((s8[7864320]{0:T(1024)(128)(4,1)}), s8[3670016]{0:T(1024)(128)(4,1)S(1)}, s32[]{:S(2)}) async-start(s8[7864320]{0:T(1024)(128)(4,1)} %bitcast.119), calls=%async_computation.3 | async-start | bytes 7340032
  134.6 7.9 %collective-permute-start.19 = (bf16[48,2560]{1,0:T(8,128)(2,1)S(1)}, bf16[48,2560]{1,0:T(8,128)(2,1)S(1)}, u32[]{:S(2)}, u32[]{:S(2)}) collective-permute-start(bf16[48,2560]{1,0:T(8,128)(2,1)S(1)} %slice.37.refs_0_), channel_id=1, source_target_pairs={{0,4},{4,8},{8,12},{12,0},{1,5},{5,9},{9,13},{13,1},{2,6},{6,10},{... | collective-permute-start | bytes 737288 | tf_op jit(solution)/shard_map/ppermute | solution.py:75
  135.8 6.7 %collective-permute-start.23 = (bf16[48,2560]{1,0:T(8,128)(2,1)S(1)}, bf16[48,2560]{1,0:T(8,128)(2,1)S(1)}, u32[]{:S(2)}, u32[]{:S(2)}) collective-permute-start(bf16[48,2560]{1,0:T(8,128)(2,1)S(1)} %slice.39.refs_4_), channel_id=1, source_target_pairs={{0,12},{4,0},{8,4},{12,8},{1,13},{5,1},{9,5},{13,9},{2,14},{6,2},{... | collective-permute-start | bytes 737288 | tf_op jit(solution)/shard_map/ppermute | solution.py:75
  137.9 12.7 %collective-permute-start.21 = (bf16[48,2560]{1,0:T(8,128)(2,1)S(1)}, bf16[48,2560]{1,0:T(8,128)(2,1)S(1)}, u32[]{:S(2)}, u32[]{:S(2)}) collective-permute-start(bf16[48,2560]{1,0:T(8,128)(2,1)S(1)} %slice.37.refs_0_), channel_id=1, source_target_pairs={{0,12},{4,0},{8,4},{12,8},{1,13},{5,1},{9,5},{13,9},{2,14},{6,2},{... | collective-permute-start | bytes 737288 | tf_op jit(solution)/shard_map/ppermute | solution.py:75
  139.4 11.3 %collective-permute-start.22 = (bf16[48,2560]{1,0:T(8,128)(2,1)S(1)}, bf16[48,2560]{1,0:T(8,128)(2,1)S(1)}, u32[]{:S(2)}, u32[]{:S(2)}) collective-permute-start(bf16[48,2560]{1,0:T(8,128)(2,1)S(1)} %slice.39.refs_4_), channel_id=1, source_target_pairs={{0,4},{4,8},{8,12},{12,0},{1,5},{5,9},{9,13},{13,1},{2,6},{6,10},{... | collective-permute-start | bytes 737288 | tf_op jit(solution)/shard_map/ppermute | solution.py:75
  142.5 10.8 %collective-permute-start.20 = (bf16[48,2560]{1,0:T(8,128)(2,1)S(1)}, bf16[48,2560]{1,0:T(8,128)(2,1)S(1)}, u32[]{:S(2)}, u32[]{:S(2)}) collective-permute-start(bf16[48,2560]{1,0:T(8,128)(2,1)S(1)} %collective-permute-done.19.refs_1_), channel_id=1, source_target_pairs={{0,4},{4,8},{8,12},{12,0},{1,5},{5,9},{9,13},{13,1},{2,6},{6,10},{... | collective-permute-start | bytes 737288 | tf_op jit(solution)/shard_map/ppermute | solution.py:75
  142.5 10.8 %collective-permute-start.24 = (bf16[48,2560]{1,0:T(8,128)(2,1)S(1)}, bf16[48,2560]{1,0:T(8,128)(2,1)S(1)}, u32[]{:S(2)}, u32[]{:S(2)}) collective-permute-start(bf16[48,2560]{1,0:T(8,128)(2,1)S(1)} %collective-permute-done.23.refs_7_), channel_id=1, source_target_pairs={{0,12},{4,0},{8,4},{12,8},{1,13},{5,1},{9,5},{13,9},{2,14},{6,2},{... | collective-permute-start | bytes 737288 | tf_op jit(solution)/shard_map/ppermute | solution.py:75
  146.3 2.9 %copy-start.1 = (bf16[32,4,40,640]{3,2,1,0:T(8,128)(2,1)S(1)}, bf16[32,4,40,640]{3,2,1,0:T(8,128)(2,1)}, u32[]{:S(2)}) copy-start(bf16[32,4,40,640]{3,2,1,0:T(8,128)(2,1)} %all-gather.4.cloned.1.call-done) | copy-start | bytes 19660804
  149.2 4.1 %copy-start = (bf16[384,1280]{1,0:T(8,128)(2,1)S(1)}, bf16[384,1280]{1,0:T(8,128)(2,1)}, u32[]{:S(2)}) copy-start(bf16[384,1280]{1,0:T(8,128)(2,1)} %get-tuple-element.16.refs_8_) | copy-start | bytes 2949124
  158.3 3.5 %collective-permute-start.26 = (bf16[4,96,320]{2,1,0:T(8,128)(2,1)S(1)}, bf16[4,96,320]{2,1,0:T(8,128)(2,1)S(1)}, u32[]{:S(2)}, u32[]{:S(2)}) collective-permute-start(bf16[4,96,320]{2,1,0:T(8,128)(2,1)S(1)} %get-tuple-element.64), channel_id=1, source_target_pairs={{0,1},{1,0},{2,3},{3,2},{4,5},{5,4},{6,7},{7,6},{8,9},{9,8},{10,11... | collective-permute-start | bytes 737288 | tf_op jit(solution)/shard_map/ppermute | solution.py:373
  160.1 8.6 %collective-permute-start.27 = (bf16[4,96,320]{2,1,0:T(8,128)(2,1)S(1)}, bf16[4,96,320]{2,1,0:T(8,128)(2,1)S(1)}, u32[]{:S(2)}, u32[]{:S(2)}) collective-permute-start(bf16[4,96,320]{2,1,0:T(8,128)(2,1)S(1)} %get-tuple-element.62), channel_id=1, source_target_pairs={{0,2},{1,3},{2,0},{3,1},{4,6},{5,7},{6,4},{7,5},{8,10},{9,11},{10,... | collective-permute-start | bytes 737288 | tf_op jit(solution)/shard_map/ppermute | solution.py:373
  160.1 15.1 %collective-permute-start.28 = (bf16[4,96,320]{2,1,0:T(8,128)(2,1)S(1)}, bf16[4,96,320]{2,1,0:T(8,128)(2,1)S(1)}, u32[]{:S(2)}, u32[]{:S(2)}) collective-permute-start(bf16[4,96,320]{2,1,0:T(8,128)(2,1)S(1)} %get-tuple-element.63), channel_id=1, source_target_pairs={{0,3},{1,2},{2,1},{3,0},{4,7},{5,6},{6,5},{7,4},{8,11},{9,10},{10,... | collective-permute-start | bytes 737288 | tf_op jit(solution)/shard_map/ppermute | solution.py:373
Sparse Core Ops, SparseCore 0:
  31.6 49.0 all-gather.5
  83.5 62.8 all-gather.3
where the time goes:
time: 184 us
  waiting for transfers between devices  70.4 us (38%)
  starting transfers between devices  37.7 us (20%)
  Pallas kernels  20.4 us (11%)
  local copies, waits for them, and re-layouts  16.5 us (9%)
  other arithmetic  14.5 us (8%)
  between operations  14.5 us (8%)
  matrix products  10 us (5%)
    ppermute x6, waiting for transfers between devices, plane_permute(): return lax.ppermute(array, AXES, plane_pairs(phase, shift))  33.6 us
    ppermute x12, starting transfers between devices, z_permute(): return lax.ppermute(array, 'z', [(j, (j + shift) % 4) for j in range(4)])  18.2 us
    ppermute x6, waiting for transfers between devices, trade(): lax.ppermute(block_to(place ^ other), ('xl', 'c'), [(i, i ^ other) for i...  15.8 us
    ppermute x12, waiting for transfers between devices, z_permute(): return lax.ppermute(array, 'z', [(j, (j + shift) % 4) for j in range(4)])  12.9 us
    unnamed x48, local copies, waits for them, and re-layouts  12.3 us
    pallas_call x1, Pallas kernels, project(): pl.pallas_call(project_kernel, out_shape=[bf16(ROWS, QKV_COLS)] * 4, in_s...  10.4 us
    ppermute x6, starting transfers between devices, plane_permute(): return lax.ppermute(array, AXES, plane_pairs(phase, shift))  8.52 us
    ppermute x5, waiting for transfers between devices, core_permute(): return lax.ppermute(array, 'c', [(0, 1), (1, 0)])  7.1 us
  transfers between devices with their start and end apart: 31, of which 18 were waited for; matrix products, arithmetic and copies ran while one was open for 15% of the time, Pallas kernels for 7%

commit v1 on v0

--- a/solution.py
+++ b/solution.py
@@ -98,17 +98,6 @@
     return (first,) + tuple(plane_permute(first, 1, shift) for shift in (1, 2, -1))
 
 
-def fetch(piece_refs, held, sems):
-    copies = [
-        pltpu.make_async_copy(piece, held.at[index // 4, index % 4], sems.at[index])
-        for index, piece in enumerate(piece_refs)
-    ]
-    for copy in copies:
-        copy.start()
-    for copy in copies:
-        copy.wait()
-
-
 def held_block(held, pos_ref, core_type, x_from, y_from, z_from):
     x_back = (pos_ref[0] - x_from) & 3
     y_back = (pos_ref[1] - y_from) & 3
@@ -122,37 +111,53 @@
 
 
 def project_kernel(pos_ref, *refs):
-    states, piece_refs, outs = refs[0], refs[1:9], refs[9:13]
-    held, weight, by_shift, sems = refs[13:]
-    fetch(piece_refs, held, sems)
-
-    def place(index, carry):
-        d, z_from, xl = index // 8, (index // 2) & 3, index & 1
-        x_from, y_from = (d // 4) * 2 + xl, d & 3
-        pair = jnp.concatenate(
-            [held_block(held, pos_ref, ct, x_from, y_from, z_from) for ct in range(2)], axis=0
+    states_ref, piece_refs, outs = refs[0], refs[1:9], refs[9:13]
+    states, held, weight, total, by_shift, sems = refs[13:]
+    loads = [
+        pltpu.make_async_copy(states_ref.at[block], states.at[block], sems.at[8 + block])
+        for block in range(4)
+    ]
+    loads += [
+        pltpu.make_async_copy(piece, held.at[index // 4, index % 4], sems.at[index])
+        for index, piece in enumerate(piece_refs)
+    ]
+    for load in loads:
+        load.start()
+    for load in loads[:4]:
+        load.wait()
+    squares = None
+    for block in range(4):
+        part = states[block].astype(jnp.float32)
+        term = jnp.sum(part * part, axis=-1, keepdims=True)
+        squares = term if squares is None else squares + term
+    factor = lax.rsqrt(squares / D + norm_epsilon)
+    for block in range(4):
+        part = states[block].astype(jnp.float32)
+        states[block] = (part * factor).astype(jnp.bfloat16)
+    for load in loads[4:]:
+        load.wait()
+    z = pos_ref[2]
+    for block in range(4):
+        for index in range(16 * block, 16 * block + 16):
+            d, z_from, xl = index // 8, (index // 2) & 3, index & 1
+            x_from, y_from = (d // 4) * 2 + xl, d & 3
+            pair = jnp.concatenate(
+                [held_block(held, pos_ref, ct, x_from, y_from, z_from) for ct in range(2)], axis=0
+            )
+            weight[index * 80 : index * 80 + 80, :] = pair.astype(jnp.bfloat16)
+        term = jnp.dot(
+            states[block],
+            weight[block * OUT_COLS : (block + 1) * OUT_COLS, :],
+            preferred_element_type=jnp.float32,
         )
-        weight[pl.ds(pl.multiple_of(index * 80, 80), 80), :] = pair.astype(jnp.bfloat16)
-        return carry
-
-    lax.fori_loop(0, 64, place, 0)
-    z = pos_ref[2]
-    for half in range(2):
-        rows = pl.ds(half * 2 * ROWS, 2 * ROWS)
-        parts = [states[block, rows, :].astype(jnp.float32) for block in range(4)]
-        total = sum(jnp.sum(part * part, axis=-1, keepdims=True) for part in parts)
-        factor = lax.rsqrt(total / D + norm_epsilon)
-        result = None
-        for block, part in enumerate(parts):
-            term = jnp.dot(
-                (part * factor).astype(jnp.bfloat16),
-                weight[block * OUT_COLS : (block + 1) * OUT_COLS, :],
-                preferred_element_type=jnp.float32,
-            )
-            result = term if result is None else result + term
-        result = result.astype(jnp.bfloat16)
-        for inner in range(2):
-            by_shift[(2 * half + inner - z) & 3] = result[inner * ROWS : (inner + 1) * ROWS]
+        if block == 0:
+            total[...] = term
+        elif block < 3:
+            total[...] += term
+        else:
+            result = (total[...] + term).astype(jnp.bfloat16)
+            for owner in range(4):
+                by_shift[(owner - z) & 3] = result[owner * ROWS : (owner + 1) * ROWS]
     for shift in range(4):
         outs[shift][...] = by_shift[shift]
 
@@ -212,15 +217,17 @@
     return pl.pallas_call(
         project_kernel,
         out_shape=[bf16(ROWS, QKV_COLS)] * 4,
-        in_specs=[SMEM_SPEC, VMEM_SPEC] + [ANY_SPEC] * 8,
+        in_specs=[SMEM_SPEC] + [ANY_SPEC] * 9,
         out_specs=[VMEM_SPEC] * 4,
         scratch_shapes=[
+            pltpu.VMEM((4, 4 * ROWS, OUT_COLS), jnp.bfloat16),
             pltpu.VMEM((2, 4, 4, 4, 40, QKV_COLS), jnp.bfloat16),
             pltpu.VMEM((D, QKV_COLS), jnp.bfloat16),
+            pltpu.VMEM((4 * ROWS, QKV_COLS), jnp.float32),
             pltpu.VMEM((4, ROWS, QKV_COLS), jnp.bfloat16),
-            pltpu.SemaphoreType.DMA((8,)),
+            pltpu.SemaphoreType.DMA((12,)),
         ],
-        compiler_params=params(40),
+        compiler_params=params(58),
         cost_estimate=cost(8 * ROWS * D * QKV_COLS, 20000000),
     )(position, states, *pieces)
 
@@ -289,63 +296,157 @@
     )(position, block, *after)
 
 
-def rotate(heads_in, cosine, sine_part):
-    half_dim = HEAD_DIM // 2
-    widened = heads_in.astype(jnp.float32)
-    front_half = widened[..., :half_dim]
-    back_half = widened[..., half_dim:]
-    return jnp.concatenate(
-        [front_half * cosine - back_half * sine_part, back_half * cosine + front_half * sine_part],
-        axis=-1,
-    ).astype(jnp.bfloat16)
-
-
-def attend(projected, key_cache, value_cache, lengths):
+PAIRS = PROMPT_DEV // 2
+STEP_PROMPTS = 8
+TALL = 2 * STEPS * GROUP
+
+
+def spread_rows(pos_ref, columns, cosine, sine_part, by_z, heads, queries, keys, values):
+    z = pos_ref[2]
+    for back in range(4):
+        by_z[(z - back) & 3] = columns[back][...]
+    for head in range(HEADS + 2 * KV_HEADS):
+        lane = (head % 7) * HEAD_DIM
+        widened = by_z[head // 7, :, lane : lane + HEAD_DIM].astype(jnp.float32)
+        if head < HEADS + KV_HEADS:
+            widened = widened * cosine[...] + pltpu.roll(widened, HEAD_DIM // 2, 1) * sine_part[...]
+            widened = widened.astype(jnp.bfloat16).astype(jnp.float32)
+        heads[head] = widened
+    for prompt in range(PROMPT_DEV):
+        pair, place = prompt // 2, (prompt % 2) * STEPS
+        rows = pl.ds(prompt, STEPS, stride=PROMPT_DEV)
+        for head in range(HEADS):
+            start = (head % GROUP) * 2 * STEPS + place
+            queries[pair, head // GROUP, start : start + STEPS, :] = heads[head, rows, :]
+        for group in range(KV_HEADS):
+            span = slice(place, place + STEPS)
+            keys[pair, group, span, :] = heads[HEADS + group, rows, :]
+            values[pair, group, span, :] = heads[HEADS + KV_HEADS + group, rows, :]
+
+
+def attend_kernel(pos_ref, length_ref, *refs):
+    columns, cosine, sine_part = refs[:4], refs[4], refs[5]
+    key_ref, value_ref, low_ref, high_ref = refs[6:10]
+    by_z, heads, queries, keys, values = refs[10:]
+    step = pl.program_id(0)
+
+    @pl.when(step == 0)
+    def _():
+        spread_rows(pos_ref, columns, cosine, sine_part, by_z, heads, queries, keys, values)
+
+    score_scale = HEAD_DIM ** (-0.5)
+    by_last = (((1,), (1,)), ((), ()))
+    row = lax.broadcasted_iota(jnp.int32, (TALL, 1), 0)
+    second = ((row >> 2) & 1) == 1
+    fresh_column = lax.broadcasted_iota(jnp.int32, (TALL, 2 * STEPS), 1)
+    fresh_mask = ((fresh_column >> 2) == ((row >> 2) & 1)) & ((fresh_column & 3) <= (row & 3))
+    column = lax.broadcasted_iota(jnp.int32, (TALL, CACHE), 1)
+    places = [(i, group) for i in range(STEP_PROMPTS // 2) for group in range(KV_HEADS)]
+    first = step * (STEP_PROMPTS // 2)
+    masks = []
+    for inner in range(STEP_PROMPTS // 2):
+        pair = first + inner
+        length = jnp.where(second, length_ref[2 * pair + 1], length_ref[2 * pair])
+        masks.append(column < length)
+    tiles = [
+        tuple(part[first + i, group].astype(jnp.bfloat16) for part in (queries, keys, values))
+        for i, group in places
+    ]
+
+    def scores(query, key):
+        return lax.dot_general(query, key, by_last, preferred_element_type=jnp.float32)
+
+    def weighted(weights, rows):
+        return jnp.dot(weights, rows, preferred_element_type=jnp.float32)
+
+    cache_scores = [
+        jnp.where(
+            second,
+            scores(query, key_ref[2 * i + 1, group]),
+            scores(query, key_ref[2 * i, group]),
+        )
+        for (i, group), (query, _, _) in zip(places, tiles)
+    ]
+    fresh_scores = [scores(query, key) for query, key, _ in tiles]
+    cache_scores = [
+        jnp.where(masks[i], part * score_scale, -1e30)
+        for (i, _), part in zip(places, cache_scores)
+    ]
+    fresh_scores = [jnp.where(fresh_mask, part * score_scale, -1e30) for part in fresh_scores]
+    largest = [
+        jnp.maximum(jnp.max(a, axis=-1, keepdims=True), jnp.max(b, axis=-1, keepdims=True))
+        for a, b in zip(cache_scores, fresh_scores)
+    ]
+    cache_exp = [jnp.exp(part - top) for part, top in zip(cache_scores, largest)]
+    fresh_exp = [jnp.exp(part - top) for part, top in zip(fresh_scores, largest)]
+    denominator = [
+        jnp.sum(a, axis=-1, keepdims=True) + jnp.sum(b, axis=-1, keepdims=True)
+        for a, b in zip(cache_exp, fresh_exp)
+    ]
+    cache_weights = [(a / total).astype(jnp.bfloat16) for a, total in zip(cache_exp, denominator)]
+    fresh_weights = [(b / total).astype(jnp.bfloat16) for b, total in zip(fresh_exp, denominator)]
+    results = [
+        jnp.where(
+            second,
+            weighted(weights, value_ref[2 * i + 1, group]),
+            weighted(weights, value_ref[2 * i, group]),
+        )
+        + weighted(fresh, tile[2])
+        for (i, group), weights, fresh, tile in zip(places, cache_weights, fresh_weights, tiles)
+    ]
+    for (i, group), result in zip(places, results):
+        queries[first + i, group] = result
+
+    @pl.when(step == pl.num_programs(0) - 1)
+    def _():
+        for prompt in range(PROMPT_DEV):
+            rows = pl.ds(prompt, STEPS, stride=PROMPT_DEV)
+            for head in range(HEADS):
+                start = (head % GROUP) * 2 * STEPS + (prompt % 2) * STEPS
+                heads[head, rows, :] = queries[
+                    prompt // 2, head // GROUP, start : start + STEPS, :
+                ]
+        for head in range(HEADS):
+            lane = head * HEAD_DIM
+            result = heads[head].astype(jnp.bfloat16)
+            low_ref[:, lane : lane + HEAD_DIM] = result[: ROWS // 2]
+            high_ref[:, lane : lane + HEAD_DIM] = result[ROWS // 2 :]
+
+
+def attend(position, columns, key_cache, value_cache, lengths):
     half_dim = HEAD_DIM // 2
     frequencies = rope_base ** (-2.0 * jnp.arange(half_dim, dtype=jnp.float32) / HEAD_DIM)
     positions = lengths[None, :] + jnp.arange(STEPS, dtype=jnp.int32)[:, None]
-    angles = positions.astype(jnp.float32)[:, :, None] * frequencies
-    cosine, sine_part = jnp.cos(angles)[:, :, None, :], jnp.sin(angles)[:, :, None, :]
-    heads = projected.reshape(STEPS, PROMPT_DEV, HEADS + 2 * KV_HEADS, HEAD_DIM)
-    rotated = rotate(heads[:, :, : HEADS + KV_HEADS], cosine, sine_part)
-    queries = rotated[:, :, :HEADS].reshape(STEPS, PROMPT_DEV, KV_HEADS, GROUP, HEAD_DIM)
-    queries = queries.transpose(1, 2, 0, 3, 4).reshape(
-        PROMPT_DEV, KV_HEADS, STEPS * GROUP, HEAD_DIM
-    )
-    fresh_keys = rotated[:, :, HEADS:].transpose(1, 2, 0, 3)
-    fresh_values = heads[:, :, HEADS + KV_HEADS :].transpose(1, 2, 0, 3)
-    score_scale = HEAD_DIM ** (-0.5)
-    cache_scores = (
-        jnp.einsum("pkgd,pkld->pkgl", queries, key_cache, preferred_element_type=jnp.float32)
-        * score_scale
-    )
-    fresh_scores = (
-        jnp.einsum("pkgd,pksd->pkgs", queries, fresh_keys, preferred_element_type=jnp.float32)
-        * score_scale
-    )
-    cache_mask = (jnp.arange(CACHE)[None, :] < lengths[:, None])[:, None, None, :]
-    row_step = jnp.arange(STEPS * GROUP) // GROUP
-    fresh_mask = (jnp.arange(STEPS)[None, :] <= row_step[:, None])[None, None]
-    cache_scores = jnp.where(cache_mask, cache_scores, -1e30)
-    fresh_scores = jnp.where(fresh_mask, fresh_scores, -1e30)
-    largest = jnp.maximum(
-        jnp.max(cache_scores, axis=-1, keepdims=True), jnp.max(fresh_scores, axis=-1, keepdims=True)
-    )
-    cache_exp = jnp.exp(cache_scores - largest)
-    fresh_exp = jnp.exp(fresh_scores - largest)
-    denominator = jnp.sum(cache_exp, axis=-1, keepdims=True) + jnp.sum(
-        fresh_exp, axis=-1, keepdims=True
-    )
-    cache_weights = (cache_exp / denominator).astype(jnp.bfloat16)
-    fresh_weights = (fresh_exp / denominator).astype(jnp.bfloat16)
-    result = jnp.einsum(
-        "pkgl,pkld->pkgd", cache_weights, value_cache, preferred_element_type=jnp.float32
-    )
-    result = result + jnp.einsum(
-        "pkgs,pksd->pkgd", fresh_weights, fresh_values, preferred_element_type=jnp.float32
-    )
-    result = result.reshape(PROMPT_DEV, KV_HEADS, STEPS, GROUP, HEAD_DIM).transpose(2, 0, 1, 3, 4)
-    return result.reshape(ROWS, ATT).astype(jnp.bfloat16)
+    angles = positions.reshape(ROWS).astype(jnp.float32)[:, None] * frequencies[None, :]
+    cosine, sine_part = jnp.cos(angles), jnp.sin(angles)
+    cache_spec = pl.BlockSpec(
+        (STEP_PROMPTS, KV_HEADS, CACHE, HEAD_DIM), lambda step: (step, 0, 0, 0)
+    )
+    pair_shape = (PAIRS, KV_HEADS, 2 * STEPS, HEAD_DIM)
+    return pl.pallas_call(
+        attend_kernel,
+        grid=(PROMPT_DEV // STEP_PROMPTS,),
+        out_shape=[bf16(ROWS // 2, ATT)] * 2,
+        in_specs=[SMEM_SPEC] * 2 + [VMEM_SPEC] * 6 + [cache_spec] * 2,
+        out_specs=[pl.BlockSpec((ROWS // 2, ATT), lambda step: (0, 0))] * 2,
+        scratch_shapes=[
+            pltpu.VMEM((4, ROWS, QKV_COLS), jnp.bfloat16),
+            pltpu.VMEM((HEADS + 2 * KV_HEADS, ROWS, HEAD_DIM), jnp.float32),
+            pltpu.VMEM((PAIRS, KV_HEADS, TALL, HEAD_DIM), jnp.float32),
+            pltpu.VMEM(pair_shape, jnp.float32),
+            pltpu.VMEM(pair_shape, jnp.float32),
+        ],
+        compiler_params=params(58),
+        cost_estimate=cost(4 * ROWS * HEADS * HEAD_DIM * CACHE, 17000000),
+    )(
+        position,
+        lengths,
+        *columns,
+        jnp.concatenate([cosine, cosine], axis=-1),
+        jnp.concatenate([-sine_part, sine_part], axis=-1),
+        key_cache,
+        value_cache,
+    )
 
 
 def on_device(
@@ -418,11 +519,9 @@
     out_columns = order(gathered.reshape(2, 4, 2, 2, 4, 40, OUT_COLS // 2))
 
     columns = [projected[0]] + [z_permute(projected[shift], shift) for shift in range(1, 4)]
-    own_rows = jnp.concatenate(
-        [lax.select_n(z, *[columns[(j - i) % 4] for j in range(4)]) for i in range(4)], axis=-1
-    )
-    attended = attend(own_rows, key_cache, value_cache, prompt_lengths)
-    low_attended, high_attended = attended[: ROWS // 2], attended[ROWS // 2 :]
+    low_attended, high_attended = attend(
+        position, columns, key_cache, value_cache, prompt_lengths
+    )
     low_ring, high_ring = z_ring(low_attended, high_attended)
     blocks = project_out(
         position,

time: 184 us -> 181 us (0.984)
  Pallas kernels: 20.4 us -> 32.4 us
  matrix products: 10 us -> 0 us
  local copies, waits for them, and re-layouts: 16.5 us -> 11.1 us
  waiting for transfers between devices: 70.4 us -> 75.8 us
  other arithmetic: 14.5 us -> 10.1 us
    pallas_call x0 -> x1, Pallas kernels: none -> 11.4 us  [attend(): pl.pallas_call(attend_kernel, grid=(PROMPT_DEV // STEP_PROMPTS,), out_sha...]
    dot_general x4 -> x0, matrix products: 10 us -> none  [the longest x1 7.01 us: attend(): jnp.einsum('pkgd,pkld->pkgl', queries, key_cache, preferred_element_type=...]
    all_gather x1, waiting for transfers between devices: 0.97 us -> 8.42 us  [on_device(): gathered = lax.all_gather(both, ('xh', 'y', 'xl', 'c'))]
    unnamed x48 -> x52, local copies, waits for them, and re-layouts: 12.3 us -> 8.39 us
    ppermute x12, waiting for transfers between devices: 12.9 us -> 9.91 us  [z_permute(): return lax.ppermute(array, 'z', [(j, (j + shift) % 4) for j in range(4)])]
    reduce_sum x2 -> x0, other arithmetic: 1.93 us -> none  [the longest x1 1.74 us: attend(): jnp.sum(cache_exp, axis=-1, keepdims=True)]
  transfers between devices with their start and end apart: 31 -> 31, of which waited for: 18 -> 17; matrix products, arithmetic and copies ran while one was open for 15% -> 7% of each run, Pallas kernels for 7% -> 14%
where the time goes in v1:
time: 181 us; the launch traced here: 180 us
  waiting for transfers between devices  75.8 us (42%)
  starting transfers between devices  36.6 us (20%)
  Pallas kernels  32.4 us (18%)
  between operations  14.4 us (8%)
  local copies, waits for them, and re-layouts  11.1 us (6%)
  other arithmetic  10.1 us (6%)
    ppermute x6, waiting for transfers between devices, plane_permute(): return lax.ppermute(array, AXES, plane_pairs(phase, shift))  33.6 us
    ppermute x12, starting transfers between devices, z_permute(): return lax.ppermute(array, 'z', [(j, (j + shift) % 4) for j in range(4)])  18.4 us
    ppermute x6, waiting for transfers between devices, trade(): lax.ppermute(block_to(place ^ other), ('xl', 'c'), [(i, i ^ other) for i...  15.7 us
    pallas_call x1, Pallas kernels, attend(): pl.pallas_call(attend_kernel, grid=(PROMPT_DEV // STEP_PROMPTS,), out_sha...  11.4 us
    pallas_call x1, Pallas kernels, project(): pl.pallas_call(project_kernel, out_shape=[bf16(ROWS, QKV_COLS)] * 4, in_s...  11 us
    ppermute x12, waiting for transfers between devices, z_permute(): return lax.ppermute(array, 'z', [(j, (j + shift) % 4) for j in range(4)])  9.91 us
    ppermute x6, starting transfers between devices, plane_permute(): return lax.ppermute(array, AXES, plane_pairs(phase, shift))  8.52 us
    all_gather x1, waiting for transfers between devices, on_device(): gathered = lax.all_gather(both, ('xh', 'y', 'xl', 'c'))  8.42 us
  transfers between devices with their start and end apart: 31, of which 17 were waited for; matrix products, arithmetic and copies ran while one was open for 7% of the time, Pallas kernels for 14%

profile of v1, /device:TPU:1, one launch (start us, length us, event | category | flops | bytes accessed | tf_op | source)
XLA Modules:
  0.0 180.3 jit_solution(13920665278224045013)
XLA Ops:
  7.2 1.7 copy.42
  9.2 1.5 collective-permute-start.3
  10.7 1.3 collective-permute-start.5
  12.0 0.3 collective-permute-start.4
  12.3 2.5 %fusion.7 = (bf16[20,5120]{1,0:T(8,128)(2,1)S(1)}, f32[20,5120]{1,0:T(8,128)}, f32[20,5120]{1,0:T(8,128)}) fusion(bf16[20,5120]{1,0:T(8,128)(2,1)} %param.13, bf16[20,5120]{1,0:T(8,128)(2,1)} %param.15, f32[20,5120]{1,0:T(8,128)S(1)} %copy-done.14, f32[20,5120]{1,0:T(8,128)S(1)} %copy-done.15), kind=kLoop, calls=%fused_computation.25 | loop fusion | flops 1843200 | bytes 2252800 | tf_op jit(solution)/shard_map/convert_element_type | solution.py:49
  14.8 1.5 fusion.2
  16.6 0.8 fusion.19
  17.3 1.8 collective-permute-start
  19.1 3.3 %collective-permute-start.1 = (bf16[40,1536]{1,0:T(8,128)(2,1)}, bf16[40,1536]{1,0:T(8,128)(2,1)}, u32[]{:S(2)}, u32[]{:S(2)}) collective-permute-start(bf16[40,1536]{1,0:T(8,128)(2,1)} %get-tuple-element.73), channel_id=1, source_target_pairs={{0,8},{4,12},{8,0},{12,4},{1,9},{5,13},{9,1},{13,5},{2,10},{6,14},... | collective-permute-start | bytes 368648 | tf_op jit(solution)/shard_map/ppermute | solution.py:75
  22.4 0.7 collective-permute-start.2
  23.1 2.5 %collective-permute-done.4 = bf16[384,320]{1,0:T(8,128)(2,1)} collective-permute-done((bf16[384,320]{1,0:T(8,128)(2,1)S(1)}, bf16[384,320]{1,0:T(8,128)(2,1)}, u32[]{:S(2)}, u32[]{:S(2)}) %collective-permute-start.4) | collective-permute-done | bytes 245792 | tf_op jit(solution)/shard_map/ppermute | solution.py:474
  25.6 1.3 fusion.17
  26.9 1.9 %concatenate.37.refs_4_ = bf16[384,1280]{1,0:T(8,128)(2,1)} concatenate(bf16[384,320]{1,0:T(8,128)(2,1)S(1)} %get-tuple-element.63, bf16[384,320]{1,0:T(8,128)(2,1)S(1)} %get-tuple-element.62, bf16[384,320]{1,0:T(8,128)(2,1)S(1)} %get-tuple-element.61, bf16[384,320]{1,0:T(8,128)(2,1)S(1)} %get-tuple-element.60), dimensions={1} | concatenate | bytes 1966080 | tf_op jit(solution)/shard_map/concatenate | solution.py:490
  28.9 0.6 copy-done.22
  29.5 1.9 %shard_map.171 = (bf16[4,40,896]{2,1,0:T(8,128)(2,1)}, bf16[4,40,640]{2,1,0:T(8,128)(2,1)}, bf16[384,1280]{1,0:T(8,128)(2,1)}) custom-call(bf16[40,1536]{1,0:T(8,128)(2,1)} %get-tuple-element.71.refs_0_, bf16[40,1536]{1,0:T(8,128)(2,1)} %copy-done.22, bf16[40,1536]{1,0:T(8,128)(2,1)} %collective-permute-done.1.refs_2_, ...), custom_call_target="tpu_custom_call", output_to_operand_aliasing={{2}: (4, {})} | custom-call | tf_op jit(solution)/shard_map/pallas_call | solution.py:268
  31.5 2.9 %collective-permute-start.8 = (bf16[4,40,896]{2,1,0:T(8,128)(2,1)}, bf16[4,40,896]{2,1,0:T(8,128)(2,1)S(1)}, u32[]{:S(2)}, u32[]{:S(2)}) collective-permute-start(bf16[4,40,896]{2,1,0:T(8,128)(2,1)} %get-tuple-element.19), channel_id=1, source_target_pairs={{0,66},{1,49},{4,70},{5,53},{8,74},{9,57},{12,78},{13,61},{16,82},... | collective-permute-start | bytes 860168 | tf_op jit(solution)/shard_map/ppermute | solution.py:71
  34.4 0.3 collective-permute-start.7
  34.7 0.7 collective-permute-start.6
  35.4 5.9 %collective-permute-done.8 = bf16[4,40,896]{2,1,0:T(8,128)(2,1)S(1)} collective-permute-done((bf16[4,40,896]{2,1,0:T(8,128)(2,1)}, bf16[4,40,896]{2,1,0:T(8,128)(2,1)S(1)}, u32[]{:S(2)}, u32[]{:S(2)}) %collective-permute-start.8) | collective-permute-done | bytes 286752 | tf_op jit(solution)/shard_map/ppermute | solution.py:71
  41.3 0.6 collective-permute-done.7
  41.9 3.0 %collective-permute-done.6 = bf16[4,40,896]{2,1,0:T(8,128)(2,1)S(1)} collective-permute-done((bf16[4,40,896]{2,1,0:T(8,128)(2,1)}, bf16[4,40,896]{2,1,0:T(8,128)(2,1)S(1)}, u32[]{:S(2)}, u32[]{:S(2)}) %collective-permute-start.6) | collective-permute-done | bytes 286752 | tf_op jit(solution)/shard_map/ppermute | solution.py:71
  45.1 1.0 collective-permute-start.9
  46.1 2.5 %collective-permute-start.10 = (bf16[4,4,40,896]{3,2,1,0:T(8,128)(2,1)S(1)}, bf16[4,4,40,896]{3,2,1,0:T(8,128)(2,1)S(1)}, u32[]{:S(2)}, u32[]{:S(2)}) collective-permute-start(bf16[4,4,40,896]{3,2,1,0:T(8,128)(2,1)S(1)} %pad_maximum_fusion.refs_1_), channel_id=1, source_target_pairs={{0,32},{1,65},{4,36},{5,69},{8,40},{9,73},{12,44},{13,77},{16,48},... | collective-permute-start | bytes 3440648 | tf_op jit(solution)/shard_map/ppermute | solution.py:71
  48.6 1.2 collective-permute-start.11
  49.7 0.6 pad_add_fusion.pos_ref
  50.3 11.2 %collective-permute-done.9.refs_2_.refs_0_ = bf16[4,4,40,896]{3,2,1,0:T(8,128)(2,1)S(1)} collective-permute-done((bf16[4,4,40,896]{3,2,1,0:T(8,128)(2,1)S(1)}, bf16[4,4,40,896]{3,2,1,0:T(8,128)(2,1)S(1)}, u32[]{:S(2)}, u32[]{:S(2)}) %collective-permute-start.9) | collective-permute-done | bytes 1146912 | tf_op jit(solution)/shard_map/ppermute | solution.py:71
  61.5 12.9 %collective-permute-done.10.refs_3_.refs_1_ = bf16[4,4,40,896]{3,2,1,0:T(8,128)(2,1)S(1)} collective-permute-done((bf16[4,4,40,896]{3,2,1,0:T(8,128)(2,1)S(1)}, bf16[4,4,40,896]{3,2,1,0:T(8,128)(2,1)S(1)}, u32[]{:S(2)}, u32[]{:S(2)}) %collective-permute-start.10) | collective-permute-done | bytes 1146912 | tf_op jit(solution)/shard_map/ppermute | solution.py:71
  74.4 1.0 copy-done.7
  75.4 1.7 shard_map.174
  77.2 3.2 %collective-permute-start.25 = (bf16[4,20,640]{2,1,0:T(8,128)(2,1)}, bf16[4,20,640]{2,1,0:T(8,128)(2,1)S(1)}, u32[]{:S(2)}, u32[]{:S(2)}) collective-permute-start(bf16[4,20,640]{2,1,0:T(8,128)(2,1)} %get-tuple-element.28), channel_id=1, source_target_pairs={{0,1},{1,0},{2,3},{3,2},{4,5},{5,4},{6,7},{7,6},{8,9},{9,8},{10,11... | collective-permute-start | bytes 307208 | tf_op jit(solution)/shard_map/ppermute | solution.py:79
  80.4 1.2 collective-permute-done.25
  81.6 1.7 maximum_select_fusion
  83.4 0.4 collective-permute-start.12
  83.9 0.4 collective-permute-start.14
  84.6 1.8 collective-permute-done.12.refs_5_
  86.4 3.4 %collective-permute-done.13.refs_6_ = bf16[4,4,40,896]{3,2,1,0:T(8,128)(2,1)S(1)} collective-permute-done((bf16[4,4,40,896]{3,2,1,0:T(8,128)(2,1)}, bf16[4,4,40,896]{3,2,1,0:T(8,128)(2,1)S(1)}, u32[]{:S(2)}, u32[]{:S(2)}) %collective-permute-start.13) | collective-permute-done | bytes 1146912 | tf_op jit(solution)/shard_map/ppermute | solution.py:79
  89.9 1.6 collective-permute-done.15.refs_8_
  91.5 11.0 %shard_map.172 = (bf16[96,896]{1,0:T(8,128)(2,1)}, bf16[96,896]{1,0:T(8,128)(2,1)}, bf16[96,896]{1,0:T(8,128)(2,1)}, bf16[96,896]{1,0:T(8,128)(2,1)}) custom-call(s32[4]{0:T(128)} %pad_add_fusion.pos_ref, bf16[4,384,1280]{2,1,0:T(8,128)(2,1)} %bitcast.84, bf16[4,4,40,896]{3,2,1,0:T(8,128)(2,1)} %copy-done.5, bf16[4,4,40,896]{3,2,1,0:T(8,128)(2,1)} %copy-done.6, ...), custom_call_target="tpu_custom_call" | custom-call | flops 3523215360 | bytes 20000000 | tf_op jit(solution)/shard_map/pallas_call | solution.py:217
  102.5 1.7 collective-permute-start.16
  104.2 3.3 %collective-permute-start.17 = (bf16[96,896]{1,0:T(8,128)(2,1)}, bf16[96,896]{1,0:T(8,128)(2,1)S(1)}, u32[]{:S(2)}, u32[]{:S(2)}) collective-permute-start(bf16[96,896]{1,0:T(8,128)(2,1)} %get-tuple-element.22), channel_id=1, source_target_pairs={{0,8},{4,12},{8,0},{12,4},{1,9},{5,13},{9,1},{13,5},{2,10},{6,14},... | collective-permute-start | bytes 516104 | tf_op jit(solution)/shard_map/ppermute | solution.py:75
  107.5 0.7 collective-permute-start.18
  108.3 0.2 fusion.26
  108.5 0.7 pad_maximum_fusion.1
  109.3 1.7 collective-permute-done.16.refs_1_
  111.0 4.5 %collective-permute-done.17.refs_2_ = bf16[96,896]{1,0:T(8,128)(2,1)S(1)} collective-permute-done((bf16[96,896]{1,0:T(8,128)(2,1)}, bf16[96,896]{1,0:T(8,128)(2,1)S(1)}, u32[]{:S(2)}, u32[]{:S(2)}) %collective-permute-start.17) | collective-permute-done | bytes 172064 | tf_op jit(solution)/shard_map/ppermute | solution.py:75
  115.6 0.7 copy-done.20
  116.3 11.4 %shard_map.173 = (bf16[48,2560]{1,0:T(8,128)(2,1)}, bf16[48,2560]{1,0:T(8,128)(2,1)}) custom-call(s32[4]{0:T(128)} %pad_add_fusion.pos_ref, s32[24]{0:T(128)} %length_ref.1, bf16[96,896]{1,0:T(8,128)(2,1)} %get-tuple-element.20.refs_0_, bf16[96,896]{1,0:T(8,128)(2,1)} %copy-done.19, bf16[96,896]{1,0:T(8,128)(2,1)} %copy-done.20, bf16[96,896]{1,0:T(8,128)(2,1)} %copy-done.21, ...), custom_call_target="tpu_custom_call" | custom-call | flops 314572800 | bytes 17000000 | tf_op jit(solution)/shard_map/pallas_call | solution.py:426
  127.8 1.2 collective-permute-start.19
  128.9 1.5 collective-permute-start.23
  130.4 1.3 collective-permute-start.21
  131.9 3.6 %collective-permute-done.19.refs_1_ = bf16[48,2560]{1,0:T(8,128)(2,1)S(1)} collective-permute-done((bf16[48,2560]{1,0:T(8,128)(2,1)}, bf16[48,2560]{1,0:T(8,128)(2,1)S(1)}, u32[]{:S(2)}, u32[]{:S(2)}) %collective-permute-start.19) | collective-permute-done | bytes 245792 | tf_op jit(solution)/shard_map/ppermute | solution.py:75
  135.5 0.3 collective-permute-start.20
  135.8 2.3 %collective-permute-start.24 = (bf16[48,2560]{1,0:T(8,128)(2,1)S(1)}, bf16[48,2560]{1,0:T(8,128)(2,1)S(1)}, u32[]{:S(2)}, u32[]{:S(2)}) collective-permute-start(bf16[48,2560]{1,0:T(8,128)(2,1)S(1)} %collective-permute-done.23.refs_7_), channel_id=1, source_target_pairs={{0,12},{4,0},{8,4},{12,8},{1,13},{5,1},{9,5},{13,9},{2,14},{6,2},{... | collective-permute-start | bytes 737288 | tf_op jit(solution)/shard_map/ppermute | solution.py:75
  138.2 8.4 %all-gather.4.cloned.1.call-done = bf16[32,4,40,640]{3,2,1,0:T(8,128)(2,1)} async-done(((bf16[1,4,40,640]{3,2,1,0:T(8,128)(2,1)}), bf16[32,4,40,640]{3,2,1,0:T(8,128)(2,1)}) %all-gather.4.cloned.1.call-update) | async-done | bytes 6553616 | tf_op jit(solution)/shard_map/all_gather | solution.py:518
  146.6 2.9 %copy-done.1 = bf16[32,4,40,640]{3,2,1,0:T(8,128)(2,1)S(1)} copy-done((bf16[32,4,40,640]{3,2,1,0:T(8,128)(2,1)S(1)}, bf16[32,4,40,640]{3,2,1,0:T(8,128)(2,1)}, u32[]{:S(2)}) %copy-start.1) | copy-done | bytes 6553624
  149.5 1.5 shard_map.175.refs_9_
  151.0 4.9 %shard_map.176 = bf16[4,4,96,320]{3,2,1,0:T(8,128)(2,1)S(1)} custom-call(s32[4]{0:T(128)S(1)} %copy-done.4, bf16[48,2560]{1,0:T(8,128)(2,1)S(1)} %copy-done.2, bf16[48,2560]{1,0:T(8,128)(2,1)S(1)} %collective-permute-done.19.refs_1_, bf16[48,2560]{1,0:T(8,128)(2,1)S(1)} %collective-permute-done.20.refs_2_, ...), custom_call_target="tpu_custom_call" | custom-call | flops 2516582400 | bytes 12000000 | tf_op jit(solution)/shard_map/pallas_call | solution.py:251
  156.0 0.4 collective-permute-start.26
  156.4 1.1 collective-permute-start.27
  157.5 0.7 collective-permute-start.28
  158.2 6.5 %collective-permute-done.27 = bf16[4,96,320]{2,1,0:T(8,128)(2,1)S(1)} collective-permute-done((bf16[4,96,320]{2,1,0:T(8,128)(2,1)S(1)}, bf16[4,96,320]{2,1,0:T(8,128)(2,1)S(1)}, u32[]{:S(2)}, u32[]{:S(2)}) %collective-permute-start.27) | collective-permute-done | bytes 245792 | tf_op jit(solution)/shard_map/ppermute | solution.py:474
  164.7 6.7 %collective-permute-done.28 = bf16[4,96,320]{2,1,0:T(8,128)(2,1)S(1)} collective-permute-done((bf16[4,96,320]{2,1,0:T(8,128)(2,1)S(1)}, bf16[4,96,320]{2,1,0:T(8,128)(2,1)S(1)}, u32[]{:S(2)}, u32[]{:S(2)}) %collective-permute-start.28) | collective-permute-done | bytes 245792 | tf_op jit(solution)/shard_map/ppermute | solution.py:474
  171.6 0.3 maximum_bitcast_fusion
  172.0 1.4 copy.45
  (81 shorter events, 2.2 us)
Async XLA Ops:
  7.2 84.3 %all-gather.6.cloned.1.call-start = ((), (), s32[]{:S(2)}) async-start(), calls=%async_computation.1 | async-start | bytes 4915200 | tf_op jit(solution)/shard_map/all_gather | solution.py:506
  9.1 3.2 %copy-start.14 = (f32[20,5120]{1,0:T(8,128)S(1)}, f32[20,5120]{1,0:T(8,128)}, u32[]{:S(2)}) copy-start(f32[20,5120]{1,0:T(8,128)} %param.17) | copy-start | bytes 1228804
  9.1 3.2 %copy-start.15 = (f32[20,5120]{1,0:T(8,128)S(1)}, f32[20,5120]{1,0:T(8,128)}, u32[]{:S(2)}) copy-start(f32[20,5120]{1,0:T(8,128)} %param.19) | copy-start | bytes 1228804
  9.2 13.2 %collective-permute-start.3 = (bf16[384,320]{1,0:T(8,128)(2,1)S(1)}, bf16[384,320]{1,0:T(8,128)(2,1)}, u32[]{:S(2)}, u32[]{:S(2)}) collective-permute-start(bf16[384,320]{1,0:T(8,128)(2,1)S(1)} %get-tuple-element.69), channel_id=1, source_target_pairs={{0,1},{1,0},{2,3},{3,2},{4,5},{5,4},{6,7},{7,6},{8,9},{9,8},{10,11... | collective-permute-start | bytes 737288 | tf_op jit(solution)/shard_map/ppermute | solution.py:474
  10.7 12.4 %collective-permute-start.5 = (bf16[384,320]{1,0:T(8,128)(2,1)S(1)}, bf16[384,320]{1,0:T(8,128)(2,1)}, u32[]{:S(2)}, u32[]{:S(2)}) collective-permute-start(bf16[384,320]{1,0:T(8,128)(2,1)S(1)} %get-tuple-element.67), channel_id=1, source_target_pairs={{0,3},{1,2},{2,1},{3,0},{4,7},{5,6},{6,5},{7,4},{8,11},{9,10},{10,... | collective-permute-start | bytes 737288 | tf_op jit(solution)/shard_map/ppermute | solution.py:474
  12.0 2.8 %copy-start.12 = (f32[40,3584]{1,0:T(8,128)S(1)}, f32[40,3584]{1,0:T(8,128)}, u32[]{:S(2)}) copy-start(f32[40,3584]{1,0:T(8,128)} %param.16) | copy-start | bytes 1720324
  12.0 2.8 %copy-start.13 = (f32[40,3584]{1,0:T(8,128)S(1)}, f32[40,3584]{1,0:T(8,128)}, u32[]{:S(2)}) copy-start(f32[40,3584]{1,0:T(8,128)} %param.18) | copy-start | bytes 1720324
  12.0 2.8 %copy-start.16 = (bf16[40,3584]{1,0:T(8,128)(2,1)S(1)}, bf16[40,3584]{1,0:T(8,128)(2,1)}, u32[]{:S(2)}) copy-start(bf16[40,3584]{1,0:T(8,128)(2,1)} %param.12) | copy-start | bytes 860164
  12.0 2.8 %copy-start.17 = (bf16[40,3584]{1,0:T(8,128)(2,1)S(1)}, bf16[40,3584]{1,0:T(8,128)(2,1)}, u32[]{:S(2)}) copy-start(bf16[40,3584]{1,0:T(8,128)(2,1)} %param.14) | copy-start | bytes 860164
  12.0 13.6 %collective-permute-start.4 = (bf16[384,320]{1,0:T(8,128)(2,1)S(1)}, bf16[384,320]{1,0:T(8,128)(2,1)}, u32[]{:S(2)}, u32[]{:S(2)}) collective-permute-start(bf16[384,320]{1,0:T(8,128)(2,1)S(1)} %get-tuple-element.68), channel_id=1, source_target_pairs={{0,2},{1,3},{2,0},{3,1},{4,6},{5,7},{6,4},{7,5},{8,10},{9,11},{10,... | collective-permute-start | bytes 737288 | tf_op jit(solution)/shard_map/ppermute | solution.py:474
  14.8 1.5 copy-start.11
  16.3 1.0 copy-start.10
  17.3 11.5 %collective-permute-start = (bf16[40,1536]{1,0:T(8,128)(2,1)}, bf16[40,1536]{1,0:T(8,128)(2,1)S(1)}, u32[]{:S(2)}, u32[]{:S(2)}) collective-permute-start(bf16[40,1536]{1,0:T(8,128)(2,1)} %get-tuple-element.72), channel_id=1, source_target_pairs={{0,4},{4,8},{8,12},{12,0},{1,5},{5,9},{9,13},{13,1},{2,6},{6,10},{... | collective-permute-start | bytes 368648 | tf_op jit(solution)/shard_map/ppermute | solution.py:75
  19.1 9.7 %collective-permute-start.1 = (bf16[40,1536]{1,0:T(8,128)(2,1)}, bf16[40,1536]{1,0:T(8,128)(2,1)}, u32[]{:S(2)}, u32[]{:S(2)}) collective-permute-start(bf16[40,1536]{1,0:T(8,128)(2,1)} %get-tuple-element.73), channel_id=1, source_target_pairs={{0,8},{4,12},{8,0},{12,4},{1,9},{5,13},{9,1},{13,5},{2,10},{6,14},... | collective-permute-start | bytes 368648 | tf_op jit(solution)/shard_map/ppermute | solution.py:75
  22.4 6.4 %collective-permute-start.2 = (bf16[40,1536]{1,0:T(8,128)(2,1)S(1)}, bf16[40,1536]{1,0:T(8,128)(2,1)S(1)}, u32[]{:S(2)}, u32[]{:S(2)}) collective-permute-start(bf16[40,1536]{1,0:T(8,128)(2,1)S(1)} %get-tuple-element.70), channel_id=1, source_target_pairs={{0,12},{4,0},{8,4},{12,8},{1,13},{5,1},{9,5},{13,9},{2,14},{6,2},{... | collective-permute-start | bytes 368648 | tf_op jit(solution)/shard_map/ppermute | solution.py:75
  28.8 0.7 copy-start.22
  28.8 0.7 copy-start.23
  31.4 13.5 %copy-start.18 = (bf16[4,40,896]{2,1,0:T(8,128)(2,1)S(1)}, bf16[4,40,896]{2,1,0:T(8,128)(2,1)}, u32[]{:S(2)}) copy-start(bf16[4,40,896]{2,1,0:T(8,128)(2,1)} %get-tuple-element.19) | copy-start | bytes 860164
  31.4 115.2 %all-gather.4.cloned.1.call-start = ((), (), s32[]{:S(2)}) async-start(), calls=%async_computation | async-start | bytes 6758400 | tf_op jit(solution)/shard_map/all_gather | solution.py:518
  31.5 9.9 %collective-permute-start.8 = (bf16[4,40,896]{2,1,0:T(8,128)(2,1)}, bf16[4,40,896]{2,1,0:T(8,128)(2,1)S(1)}, u32[]{:S(2)}, u32[]{:S(2)}) collective-permute-start(bf16[4,40,896]{2,1,0:T(8,128)(2,1)} %get-tuple-element.19), channel_id=1, source_target_pairs={{0,66},{1,49},{4,70},{5,53},{8,74},{9,57},{12,78},{13,61},{16,82},... | collective-permute-start | bytes 860168 | tf_op jit(solution)/shard_map/ppermute | solution.py:71
  34.4 7.5 %collective-permute-start.7 = (bf16[4,40,896]{2,1,0:T(8,128)(2,1)}, bf16[4,40,896]{2,1,0:T(8,128)(2,1)S(1)}, u32[]{:S(2)}, u32[]{:S(2)}) collective-permute-start(bf16[4,40,896]{2,1,0:T(8,128)(2,1)} %get-tuple-element.19), channel_id=1, source_target_pairs={{0,64},{1,33},{4,68},{5,37},{8,72},{9,41},{12,76},{13,45},{16,80},... | collective-permute-start | bytes 860168 | tf_op jit(solution)/shard_map/ppermute | solution.py:71
  34.7 10.2 %collective-permute-start.6 = (bf16[4,40,896]{2,1,0:T(8,128)(2,1)}, bf16[4,40,896]{2,1,0:T(8,128)(2,1)S(1)}, u32[]{:S(2)}, u32[]{:S(2)}) collective-permute-start(bf16[4,40,896]{2,1,0:T(8,128)(2,1)} %get-tuple-element.19), channel_id=1, source_target_pairs={{0,2},{1,17},{4,6},{5,21},{8,10},{9,25},{12,14},{13,29},{16,18},{1... | collective-permute-start | bytes 860168 | tf_op jit(solution)/shard_map/ppermute | solution.py:71
  45.1 38.2 %copy-start.5 = (bf16[4,4,40,896]{3,2,1,0:T(8,128)(2,1)}, bf16[4,4,40,896]{3,2,1,0:T(8,128)(2,1)S(1)}, u32[]{:S(2)}) copy-start(bf16[4,4,40,896]{3,2,1,0:T(8,128)(2,1)S(1)} %pad_maximum_fusion.refs_1_) | copy-start | bytes 3440644
  45.1 16.4 %collective-permute-start.9 = (bf16[4,4,40,896]{3,2,1,0:T(8,128)(2,1)S(1)}, bf16[4,4,40,896]{3,2,1,0:T(8,128)(2,1)S(1)}, u32[]{:S(2)}, u32[]{:S(2)}) collective-permute-start(bf16[4,4,40,896]{3,2,1,0:T(8,128)(2,1)S(1)} %pad_maximum_fusion.refs_1_), channel_id=1, source_target_pairs={{0,16},{1,3},{4,20},{5,7},{8,24},{9,11},{12,28},{13,15},{16,32},{1... | collective-permute-start | bytes 3440648 | tf_op jit(solution)/shard_map/ppermute | solution.py:71
  46.1 28.3 %collective-permute-start.10 = (bf16[4,4,40,896]{3,2,1,0:T(8,128)(2,1)S(1)}, bf16[4,4,40,896]{3,2,1,0:T(8,128)(2,1)S(1)}, u32[]{:S(2)}, u32[]{:S(2)}) collective-permute-start(bf16[4,4,40,896]{3,2,1,0:T(8,128)(2,1)S(1)} %pad_maximum_fusion.refs_1_), channel_id=1, source_target_pairs={{0,32},{1,65},{4,36},{5,69},{8,40},{9,73},{12,44},{13,77},{16,48},... | collective-permute-start | bytes 3440648 | tf_op jit(solution)/shard_map/ppermute | solution.py:71
  48.6 25.9 %collective-permute-start.11 = (bf16[4,4,40,896]{3,2,1,0:T(8,128)(2,1)S(1)}, bf16[4,4,40,896]{3,2,1,0:T(8,128)(2,1)}, u32[]{:S(2)}, u32[]{:S(2)}) collective-permute-start(bf16[4,4,40,896]{3,2,1,0:T(8,128)(2,1)S(1)} %pad_maximum_fusion.refs_1_), channel_id=1, source_target_pairs={{0,48},{1,67},{4,52},{5,71},{8,56},{9,75},{12,60},{13,79},{16,0},{... | collective-permute-start | bytes 3440648 | tf_op jit(solution)/shard_map/ppermute | solution.py:71
  61.5 12.9 %copy-start.6 = (bf16[4,4,40,896]{3,2,1,0:T(8,128)(2,1)}, bf16[4,4,40,896]{3,2,1,0:T(8,128)(2,1)S(1)}, u32[]{:S(2)}) copy-start(bf16[4,4,40,896]{3,2,1,0:T(8,128)(2,1)S(1)} %collective-permute-done.9.refs_2_.refs_0_) | copy-start | bytes 3440644
  74.4 1.0 copy-start.7
  75.4 9.0 %copy-start.24 = (s32[24]{0:T(128)S(1)}, s32[24]{0:T(128)}, u32[]{:S(2)}) copy-start(s32[24]{0:T(128)} %length_ref.1) | copy-start | bytes 292
  77.2 4.4 %collective-permute-start.25 = (bf16[4,20,640]{2,1,0:T(8,128)(2,1)}, bf16[4,20,640]{2,1,0:T(8,128)(2,1)S(1)}, u32[]{:S(2)}, u32[]{:S(2)}) collective-permute-start(bf16[4,20,640]{2,1,0:T(8,128)(2,1)} %get-tuple-element.28), channel_id=1, source_target_pairs={{0,1},{1,0},{2,3},{3,2},{4,5},{5,4},{6,7},{7,6},{8,9},{9,8},{10,11... | collective-permute-start | bytes 307208 | tf_op jit(solution)/shard_map/ppermute | solution.py:79
  83.4 3.0 %collective-permute-start.12 = (bf16[4,4,40,896]{3,2,1,0:T(8,128)(2,1)S(1)}, bf16[4,4,40,896]{3,2,1,0:T(8,128)(2,1)S(1)}, u32[]{:S(2)}, u32[]{:S(2)}) collective-permute-start(bf16[4,4,40,896]{3,2,1,0:T(8,128)(2,1)S(1)} %pad_maximum_fusion.refs_1_), channel_id=1, source_target_pairs={{0,1},{1,0},{2,3},{3,2},{4,5},{5,4},{6,7},{7,6},{8,9},{9,8},{10,11... | collective-permute-start | bytes 3440648 | tf_op jit(solution)/shard_map/ppermute | solution.py:79
  83.8 5.9 %collective-permute-start.13 = (bf16[4,4,40,896]{3,2,1,0:T(8,128)(2,1)}, bf16[4,4,40,896]{3,2,1,0:T(8,128)(2,1)S(1)}, u32[]{:S(2)}, u32[]{:S(2)}) collective-permute-start(bf16[4,4,40,896]{3,2,1,0:T(8,128)(2,1)} %copy-done.6), channel_id=1, source_target_pairs={{0,1},{1,0},{2,3},{3,2},{4,5},{5,4},{6,7},{7,6},{8,9},{9,8},{10,11... | collective-permute-start | bytes 3440648 | tf_op jit(solution)/shard_map/ppermute | solution.py:79
  83.9 5.9 %collective-permute-start.14 = (bf16[4,4,40,896]{3,2,1,0:T(8,128)(2,1)}, bf16[4,4,40,896]{3,2,1,0:T(8,128)(2,1)}, u32[]{:S(2)}, u32[]{:S(2)}) collective-permute-start(bf16[4,4,40,896]{3,2,1,0:T(8,128)(2,1)} %copy-done.7), channel_id=1, source_target_pairs={{0,1},{1,0},{2,3},{3,2},{4,5},{5,4},{6,7},{7,6},{8,9},{9,8},{10,11... | collective-permute-start | bytes 3440648 | tf_op jit(solution)/shard_map/ppermute | solution.py:79
  84.3 7.2 %collective-permute-start.15 = (bf16[4,4,40,896]{3,2,1,0:T(8,128)(2,1)}, bf16[4,4,40,896]{3,2,1,0:T(8,128)(2,1)}, u32[]{:S(2)}, u32[]{:S(2)}) collective-permute-start(bf16[4,4,40,896]{3,2,1,0:T(8,128)(2,1)} %collective-permute-done.11.refs_4_.refs_2_), channel_id=1, source_target_pairs={{0,1},{1,0},{2,3},{3,2},{4,5},{5,4},{6,7},{7,6},{8,9},{9,8},{10,11... | collective-permute-start | bytes 3440648 | tf_op jit(solution)/shard_map/ppermute | solution.py:79
  86.4 5.1 %copy-start.8 = (bf16[4,4,40,896]{3,2,1,0:T(8,128)(2,1)}, bf16[4,4,40,896]{3,2,1,0:T(8,128)(2,1)S(1)}, u32[]{:S(2)}) copy-start(bf16[4,4,40,896]{3,2,1,0:T(8,128)(2,1)S(1)} %collective-permute-done.12.refs_5_) | copy-start | bytes 3440644
  89.7 1.8 copy-start.9
  102.5 8.5 %collective-permute-start.16 = (bf16[96,896]{1,0:T(8,128)(2,1)}, bf16[96,896]{1,0:T(8,128)(2,1)S(1)}, u32[]{:S(2)}, u32[]{:S(2)}) collective-permute-start(bf16[96,896]{1,0:T(8,128)(2,1)} %get-tuple-element.21), channel_id=1, source_target_pairs={{0,4},{4,8},{8,12},{12,0},{1,5},{5,9},{9,13},{13,1},{2,6},{6,10},{... | collective-permute-start | bytes 516104 | tf_op jit(solution)/shard_map/ppermute | solution.py:75
  104.2 11.3 %collective-permute-start.17 = (bf16[96,896]{1,0:T(8,128)(2,1)}, bf16[96,896]{1,0:T(8,128)(2,1)S(1)}, u32[]{:S(2)}, u32[]{:S(2)}) collective-permute-start(bf16[96,896]{1,0:T(8,128)(2,1)} %get-tuple-element.22), channel_id=1, source_target_pairs={{0,8},{4,12},{8,0},{12,4},{1,9},{5,13},{9,1},{13,5},{2,10},{6,14},... | collective-permute-start | bytes 516104 | tf_op jit(solution)/shard_map/ppermute | solution.py:75
  107.5 8.0 %collective-permute-start.18 = (bf16[96,896]{1,0:T(8,128)(2,1)}, bf16[96,896]{1,0:T(8,128)(2,1)S(1)}, u32[]{:S(2)}, u32[]{:S(2)}) collective-permute-start(bf16[96,896]{1,0:T(8,128)(2,1)} %get-tuple-element.23), channel_id=1, source_target_pairs={{0,12},{4,0},{8,4},{12,8},{1,13},{5,1},{9,5},{13,9},{2,14},{6,2},{... | collective-permute-start | bytes 516104 | tf_op jit(solution)/shard_map/ppermute | solution.py:75
  111.0 4.6 %copy-start.19 = (bf16[96,896]{1,0:T(8,128)(2,1)}, bf16[96,896]{1,0:T(8,128)(2,1)S(1)}, u32[]{:S(2)}) copy-start(bf16[96,896]{1,0:T(8,128)(2,1)S(1)} %collective-permute-done.16.refs_1_) | copy-start | bytes 516100
  115.6 0.7 copy-start.20
  115.6 0.7 copy-start.21
  127.8 7.7 %collective-permute-start.19 = (bf16[48,2560]{1,0:T(8,128)(2,1)}, bf16[48,2560]{1,0:T(8,128)(2,1)S(1)}, u32[]{:S(2)}, u32[]{:S(2)}) collective-permute-start(bf16[48,2560]{1,0:T(8,128)(2,1)} %get-tuple-element.24.refs_0_), channel_id=1, source_target_pairs={{0,4},{4,8},{8,12},{12,0},{1,5},{5,9},{9,13},{13,1},{2,6},{6,10},{... | collective-permute-start | bytes 737288 | tf_op jit(solution)/shard_map/ppermute | solution.py:75
  128.9 6.9 %collective-permute-start.23 = (bf16[48,2560]{1,0:T(8,128)(2,1)}, bf16[48,2560]{1,0:T(8,128)(2,1)S(1)}, u32[]{:S(2)}, u32[]{:S(2)}) collective-permute-start(bf16[48,2560]{1,0:T(8,128)(2,1)} %get-tuple-element.25.refs_4_), channel_id=1, source_target_pairs={{0,12},{4,0},{8,4},{12,8},{1,13},{5,1},{9,5},{13,9},{2,14},{6,2},{... | collective-permute-start | bytes 737288 | tf_op jit(solution)/shard_map/ppermute | solution.py:75
  130.4 20.5 %collective-permute-start.21 = (bf16[48,2560]{1,0:T(8,128)(2,1)}, bf16[48,2560]{1,0:T(8,128)(2,1)S(1)}, u32[]{:S(2)}, u32[]{:S(2)}) collective-permute-start(bf16[48,2560]{1,0:T(8,128)(2,1)} %get-tuple-element.24.refs_0_), channel_id=1, source_target_pairs={{0,12},{4,0},{8,4},{12,8},{1,13},{5,1},{9,5},{13,9},{2,14},{6,2},{... | collective-permute-start | bytes 737288 | tf_op jit(solution)/shard_map/ppermute | solution.py:75
  131.7 19.3 %collective-permute-start.22 = (bf16[48,2560]{1,0:T(8,128)(2,1)}, bf16[48,2560]{1,0:T(8,128)(2,1)S(1)}, u32[]{:S(2)}, u32[]{:S(2)}) collective-permute-start(bf16[48,2560]{1,0:T(8,128)(2,1)} %get-tuple-element.25.refs_4_), channel_id=1, source_target_pairs={{0,4},{4,8},{8,12},{12,0},{1,5},{5,9},{9,13},{13,1},{2,6},{6,10},{... | collective-permute-start | bytes 737288 | tf_op jit(solution)/shard_map/ppermute | solution.py:75
  135.5 15.5 %collective-permute-start.20 = (bf16[48,2560]{1,0:T(8,128)(2,1)S(1)}, bf16[48,2560]{1,0:T(8,128)(2,1)S(1)}, u32[]{:S(2)}, u32[]{:S(2)}) collective-permute-start(bf16[48,2560]{1,0:T(8,128)(2,1)S(1)} %collective-permute-done.19.refs_1_), channel_id=1, source_target_pairs={{0,4},{4,8},{8,12},{12,0},{1,5},{5,9},{9,13},{13,1},{2,6},{6,10},{... | collective-permute-start | bytes 737288 | tf_op jit(solution)/shard_map/ppermute | solution.py:75
  135.8 15.2 %collective-permute-start.24 = (bf16[48,2560]{1,0:T(8,128)(2,1)S(1)}, bf16[48,2560]{1,0:T(8,128)(2,1)S(1)}, u32[]{:S(2)}, u32[]{:S(2)}) collective-permute-start(bf16[48,2560]{1,0:T(8,128)(2,1)S(1)} %collective-permute-done.23.refs_7_), channel_id=1, source_target_pairs={{0,12},{4,0},{8,4},{12,8},{1,13},{5,1},{9,5},{13,9},{2,14},{6,2},{... | collective-permute-start | bytes 737288 | tf_op jit(solution)/shard_map/ppermute | solution.py:75
  146.6 2.9 %copy-start.1 = (bf16[32,4,40,640]{3,2,1,0:T(8,128)(2,1)S(1)}, bf16[32,4,40,640]{3,2,1,0:T(8,128)(2,1)}, u32[]{:S(2)}) copy-start(bf16[32,4,40,640]{3,2,1,0:T(8,128)(2,1)} %all-gather.4.cloned.1.call-done) | copy-start | bytes 19660804
  149.5 1.5 copy-start
  149.5 1.5 copy-start.2
  149.5 1.6 copy-start.3
  149.5 1.6 copy-start.4
  156.0 2.2 %collective-permute-start.26 = (bf16[4,96,320]{2,1,0:T(8,128)(2,1)S(1)}, bf16[4,96,320]{2,1,0:T(8,128)(2,1)S(1)}, u32[]{:S(2)}, u32[]{:S(2)}) collective-permute-start(bf16[4,96,320]{2,1,0:T(8,128)(2,1)S(1)} %get-tuple-element.66), channel_id=1, source_target_pairs={{0,1},{1,0},{2,3},{3,2},{4,5},{5,4},{6,7},{7,6},{8,9},{9,8},{10,11... | collective-permute-start | bytes 737288 | tf_op jit(solution)/shard_map/ppermute | solution.py:474
  156.4 8.4 %collective-permute-start.27 = (bf16[4,96,320]{2,1,0:T(8,128)(2,1)S(1)}, bf16[4,96,320]{2,1,0:T(8,128)(2,1)S(1)}, u32[]{:S(2)}, u32[]{:S(2)}) collective-permute-start(bf16[4,96,320]{2,1,0:T(8,128)(2,1)S(1)} %get-tuple-element.64), channel_id=1, source_target_pairs={{0,2},{1,3},{2,0},{3,1},{4,6},{5,7},{6,4},{7,5},{8,10},{9,11},{10,... | collective-permute-start | bytes 737288 | tf_op jit(solution)/shard_map/ppermute | solution.py:474
  157.5 13.9 %collective-permute-start.28 = (bf16[4,96,320]{2,1,0:T(8,128)(2,1)S(1)}, bf16[4,96,320]{2,1,0:T(8,128)(2,1)S(1)}, u32[]{:S(2)}, u32[]{:S(2)}) collective-permute-start(bf16[4,96,320]{2,1,0:T(8,128)(2,1)S(1)} %get-tuple-element.65), channel_id=1, source_target_pairs={{0,3},{1,2},{2,1},{3,0},{4,7},{5,6},{6,5},{7,4},{8,11},{9,10},{10,... | collective-permute-start | bytes 737288 | tf_op jit(solution)/shard_map/ppermute | solution.py:474
Sparse Core Ops, SparseCore 0:
  31.6 49.0 all-gather.5
  83.5 63.0 all-gather.3

commit v2 on v1

--- a/solution.py
+++ b/solution.py
@@ -1,3 +1,5 @@
+import functools
+
 import jax
 import jax.numpy as jnp
 from jax import lax
@@ -183,17 +185,19 @@
     lax.fori_loop(0, 32, place, 0)
 
 
-def output_kernel(pos_ref, *refs):
-    lows, highs, states, weight, out_ref = refs[:4], refs[4:8], refs[8], refs[9], refs[10]
+def output_kernel(flip, pos_ref, *refs):
+    lows, highs, states, weight, out_ref = refs[:4], refs[4:8], refs[8], refs[9], refs[-1]
     z = pos_ref[2]
+    side = (pos_ref[0] & 1) ^ flip
+    lanes = pl.ds(pl.multiple_of(side * 2 * FEATURES, 2 * FEATURES), 2 * FEATURES)
     for back in range(4):
         owner = (z - back) & 3
         part = jnp.concatenate([lows[back][...], highs[back][...]], axis=0)
-        result = jnp.dot(part, weight[...], preferred_element_type=jnp.float32)
+        result = jnp.dot(part, weight[:, lanes], preferred_element_type=jnp.float32)
         rows = pl.ds(pl.multiple_of(owner * ROWS, ROWS), ROWS)
-        result = (states[rows, :].astype(jnp.float32) + result).astype(jnp.bfloat16)
-        for block in range(4):
-            out_ref[block, owner] = result[:, block * FEATURES : (block + 1) * FEATURES]
+        result = (states[rows, lanes].astype(jnp.float32) + result).astype(jnp.bfloat16)
+        for core in range(2):
+            out_ref[core, owner] = result[:, core * FEATURES : (core + 1) * FEATURES]
 
 
 SMEM_SPEC = pl.BlockSpec(memory_space=pltpu.SMEM)
@@ -247,15 +251,15 @@
     )(halves)
 
 
-def project_out(position, lows, highs, states, weight):
+def project_out(flip, position, lows, highs, states, weight, *after):
     return pl.pallas_call(
-        output_kernel,
-        out_shape=bf16(4, 4, ROWS, FEATURES),
-        in_specs=[SMEM_SPEC] + [VMEM_SPEC] * 10,
+        functools.partial(output_kernel, flip),
+        out_shape=bf16(2, 4, ROWS, FEATURES),
+        in_specs=[SMEM_SPEC] + [VMEM_SPEC] * 10 + [ANY_SPEC] * len(after),
         out_specs=VMEM_SPEC,
         compiler_params=params(24),
-        cost_estimate=cost(8 * ROWS * ATT * OUT_COLS, 12000000),
-    )(position, *lows, *highs, states, weight)
+        cost_estimate=cost(4 * ROWS * ATT * OUT_COLS, 8000000),
+    )(position, *lows, *highs, states, weight, *after)
 
 
 def stack_kernel(*refs):
@@ -467,13 +471,11 @@
     place = xl * 2 + c
     position = jnp.stack([xh * 2 + xl, y, z, c]).astype(jnp.int32)
 
-    def trade(block_to):
-        came = [block_to(place)]
+    def trade(block_for):
+        came = [block_for(0)]
         for other in range(1, 4):
             came.append(
-                lax.ppermute(
-                    block_to(place ^ other), ("xl", "c"), [(i, i ^ other) for i in range(4)]
-                )
+                lax.ppermute(block_for(other), ("xl", "c"), [(i, i ^ other) for i in range(4)])
             )
         return [lax.select_n(place, *[came[i ^ j] for j in range(4)]) for i in range(4)]
 
@@ -486,7 +488,9 @@
 
     by_place = step_states.reshape(STEPS, 4, 4, PROMPT_DEV, FEATURES)
     by_place = by_place.transpose(2, 1, 0, 3, 4).reshape(4, 4 * ROWS, FEATURES)
-    came = trade(lambda i: lax.dynamic_index_in_dim(by_place, i, 0, keepdims=False))
+    came = trade(
+        lambda other: lax.dynamic_index_in_dim(by_place, place ^ other, 0, keepdims=False)
+    )
     own_states = jnp.concatenate(came, axis=-1)
 
     by_z = jnp.concatenate(
@@ -523,14 +527,24 @@
         position, columns, key_cache, value_cache, prompt_lengths
     )
     low_ring, high_ring = z_ring(low_attended, high_attended)
-    blocks = project_out(
+    operands = (
         position,
         (low_attended,) + low_ring,
         (high_attended,) + high_ring,
         own_states,
         out_columns,
     )
-    came = trade(lambda i: lax.dynamic_index_in_dim(blocks, i, 0, keepdims=False))
+    far_blocks = project_out(1, *operands)
+
+    def send(blocks, other):
+        block = lax.dynamic_index_in_dim(blocks, c ^ (other & 1), 0, keepdims=False)
+        return lax.ppermute(block, ("xl", "c"), [(i, i ^ other) for i in range(4)])
+
+    from_far = [send(far_blocks, other) for other in (2, 3)]
+    near_blocks = project_out(0, *operands, from_far[1])
+    own_block = lax.dynamic_index_in_dim(near_blocks, c, 0, keepdims=False)
+    came = [own_block, send(near_blocks, 1)] + from_far
+    came = [lax.select_n(place, *[came[i ^ j] for j in range(4)]) for i in range(4)]
     outputs = jnp.stack(
         [block.reshape(4, STEPS, PROMPT_DEV, FEATURES) for block in came], axis=1
     )

time: 181 us -> 179 us (0.989)
  waiting for transfers between devices: 75.8 us -> 73.1 us
    ppermute x6, waiting for transfers between devices: 15.7 us -> 12.9 us  [the longest x3 10.5 us: send(): return lax.ppermute(block, ('xl', 'c'), [(i, i ^ other) for i in range(4)])]
    pallas_call x1 -> x2, Pallas kernels: 4.85 us -> 6.03 us  [project_out(): pl.pallas_call(functools.partial(output_kernel, flip), out_shape=bf16(2,...]
  transfers between devices with their start and end apart: 31 -> 31, of which waited for: 17 -> 17; matrix products, arithmetic and copies ran while one was open for 7% -> 7% of each run, Pallas kernels for 14% -> 16%
where the time goes in v2:
time: 179 us; the launch traced here: 178 us
  waiting for transfers between devices  73.1 us (41%)
  starting transfers between devices  36.2 us (20%)
  Pallas kernels  33.5 us (19%)
  between operations  14.4 us (8%)
  local copies, waits for them, and re-layouts  11.1 us (6%)
  other arithmetic  10.1 us (6%)
    ppermute x6, waiting for transfers between devices, plane_permute(): return lax.ppermute(array, AXES, plane_pairs(phase, shift))  33.6 us
    ppermute x12, starting transfers between devices, z_permute(): return lax.ppermute(array, 'z', [(j, (j + shift) % 4) for j in range(4)])  18.4 us
    pallas_call x1, Pallas kernels, attend(): pl.pallas_call(attend_kernel, grid=(PROMPT_DEV // STEP_PROMPTS,), out_sha...  11.4 us
    pallas_call x1, Pallas kernels, project(): pl.pallas_call(project_kernel, out_shape=[bf16(ROWS, QKV_COLS)] * 4, in_s...  11 us
    ppermute x3, waiting for transfers between devices, send(): return lax.ppermute(block, ('xl', 'c'), [(i, i ^ other) for i in range(4)])  10.5 us
    ppermute x12, waiting for transfers between devices, z_permute(): return lax.ppermute(array, 'z', [(j, (j + shift) % 4) for j in range(4)])  9.91 us
    ppermute x6, starting transfers between devices, plane_permute(): return lax.ppermute(array, AXES, plane_pairs(phase, shift))  8.52 us
    all_gather x1, waiting for transfers between devices, on_device(): gathered = lax.all_gather(both, ('xh', 'y', 'xl', 'c'))  8.42 us
  transfers between devices with their start and end apart: 31, of which 17 were waited for; matrix products, arithmetic and copies ran while one was open for 7% of the time, Pallas kernels for 16%

profile of v2, /device:TPU:1, one launch (start us, length us, event | category | flops | bytes accessed | tf_op | source)
XLA Modules:
  0.0 178.3 jit_solution(12262591543227731412)
XLA Ops:
  7.2 1.7 copy.46
  9.2 1.5 collective-permute-start.3
  10.7 1.3 collective-permute-start.5
  12.0 0.3 collective-permute-start.4
  12.3 2.5 %fusion.7 = (bf16[20,5120]{1,0:T(8,128)(2,1)S(1)}, f32[20,5120]{1,0:T(8,128)}, f32[20,5120]{1,0:T(8,128)}) fusion(bf16[20,5120]{1,0:T(8,128)(2,1)} %param.13, bf16[20,5120]{1,0:T(8,128)(2,1)} %param.15, f32[20,5120]{1,0:T(8,128)S(1)} %copy-done.14, f32[20,5120]{1,0:T(8,128)S(1)} %copy-done.15), kind=kLoop, calls=%fused_computation.25 | loop fusion | flops 1843200 | bytes 2252800 | tf_op jit(solution)/shard_map/convert_element_type | solution.py:51
  14.8 1.5 fusion.2
  16.6 0.8 fusion.19
  17.3 1.8 collective-permute-start
  19.1 3.3 %collective-permute-start.1 = (bf16[40,1536]{1,0:T(8,128)(2,1)}, bf16[40,1536]{1,0:T(8,128)(2,1)}, u32[]{:S(2)}, u32[]{:S(2)}) collective-permute-start(bf16[40,1536]{1,0:T(8,128)(2,1)} %get-tuple-element.72), channel_id=1, source_target_pairs={{0,8},{4,12},{8,0},{12,4},{1,9},{5,13},{9,1},{13,5},{2,10},{6,14},... | collective-permute-start | bytes 368648 | tf_op jit(solution)/shard_map/ppermute | solution.py:77
  22.4 0.7 collective-permute-start.2
  23.1 2.5 %collective-permute-done.4 = bf16[384,320]{1,0:T(8,128)(2,1)} collective-permute-done((bf16[384,320]{1,0:T(8,128)(2,1)S(1)}, bf16[384,320]{1,0:T(8,128)(2,1)}, u32[]{:S(2)}, u32[]{:S(2)}) %collective-permute-start.4) | collective-permute-done | bytes 245792 | tf_op jit(solution)/shard_map/ppermute | solution.py:478
  25.6 1.3 fusion.17
  26.9 1.9 %concatenate.37.refs_4_ = bf16[384,1280]{1,0:T(8,128)(2,1)} concatenate(bf16[384,320]{1,0:T(8,128)(2,1)S(1)} %get-tuple-element.59, bf16[384,320]{1,0:T(8,128)(2,1)S(1)} %get-tuple-element.58, bf16[384,320]{1,0:T(8,128)(2,1)S(1)} %get-tuple-element.57, bf16[384,320]{1,0:T(8,128)(2,1)S(1)} %get-tuple-element.56), dimensions={1} | concatenate | bytes 1966080 | tf_op jit(solution)/shard_map/concatenate | solution.py:494
  28.9 0.6 copy-done.22
  29.5 1.9 %shard_map.171 = (bf16[4,40,896]{2,1,0:T(8,128)(2,1)}, bf16[4,40,640]{2,1,0:T(8,128)(2,1)}, bf16[384,1280]{1,0:T(8,128)(2,1)}) custom-call(bf16[40,1536]{1,0:T(8,128)(2,1)} %get-tuple-element.70.refs_0_, bf16[40,1536]{1,0:T(8,128)(2,1)} %copy-done.22, bf16[40,1536]{1,0:T(8,128)(2,1)} %collective-permute-done.1.refs_2_, ...), custom_call_target="tpu_custom_call", output_to_operand_aliasing={{2}: (4, {})} | custom-call | tf_op jit(solution)/shard_map/pallas_call | solution.py:272
  31.5 2.9 %collective-permute-start.8 = (bf16[4,40,896]{2,1,0:T(8,128)(2,1)}, bf16[4,40,896]{2,1,0:T(8,128)(2,1)S(1)}, u32[]{:S(2)}, u32[]{:S(2)}) collective-permute-start(bf16[4,40,896]{2,1,0:T(8,128)(2,1)} %get-tuple-element.19), channel_id=1, source_target_pairs={{0,66},{1,49},{4,70},{5,53},{8,74},{9,57},{12,78},{13,61},{16,82},... | collective-permute-start | bytes 860168 | tf_op jit(solution)/shard_map/ppermute | solution.py:73
  34.4 0.3 collective-permute-start.7
  34.7 0.7 collective-permute-start.6
  35.4 5.9 %collective-permute-done.8 = bf16[4,40,896]{2,1,0:T(8,128)(2,1)S(1)} collective-permute-done((bf16[4,40,896]{2,1,0:T(8,128)(2,1)}, bf16[4,40,896]{2,1,0:T(8,128)(2,1)S(1)}, u32[]{:S(2)}, u32[]{:S(2)}) %collective-permute-start.8) | collective-permute-done | bytes 286752 | tf_op jit(solution)/shard_map/ppermute | solution.py:73
  41.3 0.6 collective-permute-done.7
  41.9 3.0 %collective-permute-done.6 = bf16[4,40,896]{2,1,0:T(8,128)(2,1)S(1)} collective-permute-done((bf16[4,40,896]{2,1,0:T(8,128)(2,1)}, bf16[4,40,896]{2,1,0:T(8,128)(2,1)S(1)}, u32[]{:S(2)}, u32[]{:S(2)}) %collective-permute-start.6) | collective-permute-done | bytes 286752 | tf_op jit(solution)/shard_map/ppermute | solution.py:73
  45.1 1.0 collective-permute-start.9
  46.1 2.5 %collective-permute-start.10 = (bf16[4,4,40,896]{3,2,1,0:T(8,128)(2,1)S(1)}, bf16[4,4,40,896]{3,2,1,0:T(8,128)(2,1)S(1)}, u32[]{:S(2)}, u32[]{:S(2)}) collective-permute-start(bf16[4,4,40,896]{3,2,1,0:T(8,128)(2,1)S(1)} %pad_maximum_fusion.1.refs_1_), channel_id=1, source_target_pairs={{0,32},{1,65},{4,36},{5,69},{8,40},{9,73},{12,44},{13,77},{16,48},... | collective-permute-start | bytes 3440648 | tf_op jit(solution)/shard_map/ppermute | solution.py:73
  48.6 1.2 collective-permute-start.11
  49.7 0.6 pad_add_fusion.pos_ref
  50.3 11.2 %collective-permute-done.9.refs_2_.refs_0_ = bf16[4,4,40,896]{3,2,1,0:T(8,128)(2,1)S(1)} collective-permute-done((bf16[4,4,40,896]{3,2,1,0:T(8,128)(2,1)S(1)}, bf16[4,4,40,896]{3,2,1,0:T(8,128)(2,1)S(1)}, u32[]{:S(2)}, u32[]{:S(2)}) %collective-permute-start.9) | collective-permute-done | bytes 1146912 | tf_op jit(solution)/shard_map/ppermute | solution.py:73
  61.5 12.9 %collective-permute-done.10.refs_3_.refs_1_ = bf16[4,4,40,896]{3,2,1,0:T(8,128)(2,1)S(1)} collective-permute-done((bf16[4,4,40,896]{3,2,1,0:T(8,128)(2,1)S(1)}, bf16[4,4,40,896]{3,2,1,0:T(8,128)(2,1)S(1)}, u32[]{:S(2)}, u32[]{:S(2)}) %collective-permute-start.10) | collective-permute-done | bytes 1146912 | tf_op jit(solution)/shard_map/ppermute | solution.py:73
  74.4 1.0 copy-done.7
  75.4 1.7 shard_map.174
  77.2 3.2 %collective-permute-start.25 = (bf16[4,20,640]{2,1,0:T(8,128)(2,1)}, bf16[4,20,640]{2,1,0:T(8,128)(2,1)S(1)}, u32[]{:S(2)}, u32[]{:S(2)}) collective-permute-start(bf16[4,20,640]{2,1,0:T(8,128)(2,1)} %get-tuple-element.28), channel_id=1, source_target_pairs={{0,1},{1,0},{2,3},{3,2},{4,5},{5,4},{6,7},{7,6},{8,9},{9,8},{10,11... | collective-permute-start | bytes 307208 | tf_op jit(solution)/shard_map/ppermute | solution.py:81
  80.4 1.2 collective-permute-done.25
  81.6 1.7 maximum_select_fusion
  83.4 0.4 collective-permute-start.12
  83.9 0.4 collective-permute-start.14
  84.6 1.8 %collective-permute-done.12.refs_5_ = bf16[4,4,40,896]{3,2,1,0:T(8,128)(2,1)S(1)} collective-permute-done((bf16[4,4,40,896]{3,2,1,0:T(8,128)(2,1)S(1)}, bf16[4,4,40,896]{3,2,1,0:T(8,128)(2,1)S(1)}, u32[]{:S(2)}, u32[]{:S(2)}) %collective-permute-start.12) | collective-permute-done | bytes 1146912 | tf_op jit(solution)/shard_map/ppermute | solution.py:81
  86.4 3.4 %collective-permute-done.13.refs_6_ = bf16[4,4,40,896]{3,2,1,0:T(8,128)(2,1)S(1)} collective-permute-done((bf16[4,4,40,896]{3,2,1,0:T(8,128)(2,1)}, bf16[4,4,40,896]{3,2,1,0:T(8,128)(2,1)S(1)}, u32[]{:S(2)}, u32[]{:S(2)}) %collective-permute-start.13) | collective-permute-done | bytes 1146912 | tf_op jit(solution)/shard_map/ppermute | solution.py:81
  89.9 1.6 collective-permute-done.15.refs_8_
  91.5 11.0 %shard_map.172 = (bf16[96,896]{1,0:T(8,128)(2,1)}, bf16[96,896]{1,0:T(8,128)(2,1)}, bf16[96,896]{1,0:T(8,128)(2,1)}, bf16[96,896]{1,0:T(8,128)(2,1)}) custom-call(s32[4]{0:T(128)} %pad_add_fusion.pos_ref, bf16[4,384,1280]{2,1,0:T(8,128)(2,1)} %bitcast.84, bf16[4,4,40,896]{3,2,1,0:T(8,128)(2,1)} %copy-done.5, bf16[4,4,40,896]{3,2,1,0:T(8,128)(2,1)} %copy-done.6, ...), custom_call_target="tpu_custom_call" | custom-call | flops 3523215360 | bytes 20000000 | tf_op jit(solution)/shard_map/pallas_call | solution.py:221
  102.5 1.7 collective-permute-start.16
  104.2 3.3 %collective-permute-start.17 = (bf16[96,896]{1,0:T(8,128)(2,1)}, bf16[96,896]{1,0:T(8,128)(2,1)S(1)}, u32[]{:S(2)}, u32[]{:S(2)}) collective-permute-start(bf16[96,896]{1,0:T(8,128)(2,1)} %get-tuple-element.22), channel_id=1, source_target_pairs={{0,8},{4,12},{8,0},{12,4},{1,9},{5,13},{9,1},{13,5},{2,10},{6,14},... | collective-permute-start | bytes 516104 | tf_op jit(solution)/shard_map/ppermute | solution.py:77
  107.5 0.7 collective-permute-start.18
  108.3 0.2 fusion.26
  108.5 0.7 pad_maximum_fusion.2
  109.3 1.7 collective-permute-done.16.refs_1_
  111.0 4.5 %collective-permute-done.17.refs_2_ = bf16[96,896]{1,0:T(8,128)(2,1)S(1)} collective-permute-done((bf16[96,896]{1,0:T(8,128)(2,1)}, bf16[96,896]{1,0:T(8,128)(2,1)S(1)}, u32[]{:S(2)}, u32[]{:S(2)}) %collective-permute-start.17) | collective-permute-done | bytes 172064 | tf_op jit(solution)/shard_map/ppermute | solution.py:77
  115.6 0.7 copy-done.20
  116.3 11.4 %shard_map.173 = (bf16[48,2560]{1,0:T(8,128)(2,1)}, bf16[48,2560]{1,0:T(8,128)(2,1)}) custom-call(s32[4]{0:T(128)} %pad_add_fusion.pos_ref, s32[24]{0:T(128)} %length_ref.1, bf16[96,896]{1,0:T(8,128)(2,1)} %get-tuple-element.20.refs_0_, bf16[96,896]{1,0:T(8,128)(2,1)} %copy-done.19, bf16[96,896]{1,0:T(8,128)(2,1)} %copy-done.20, bf16[96,896]{1,0:T(8,128)(2,1)} %copy-done.21, ...), custom_call_target="tpu_custom_call" | custom-call | flops 314572800 | bytes 17000000 | tf_op jit(solution)/shard_map/pallas_call | solution.py:430
  127.8 1.2 collective-permute-start.19
  128.9 1.5 collective-permute-start.23
  130.4 1.2 collective-permute-start.21
  131.9 3.6 %collective-permute-done.19.refs_1_ = bf16[48,2560]{1,0:T(8,128)(2,1)S(1)} collective-permute-done((bf16[48,2560]{1,0:T(8,128)(2,1)}, bf16[48,2560]{1,0:T(8,128)(2,1)S(1)}, u32[]{:S(2)}, u32[]{:S(2)}) %collective-permute-start.19) | collective-permute-done | bytes 245792 | tf_op jit(solution)/shard_map/ppermute | solution.py:77
  135.5 0.3 collective-permute-start.20
  135.8 2.4 %collective-permute-start.24 = (bf16[48,2560]{1,0:T(8,128)(2,1)S(1)}, bf16[48,2560]{1,0:T(8,128)(2,1)S(1)}, u32[]{:S(2)}, u32[]{:S(2)}) collective-permute-start(bf16[48,2560]{1,0:T(8,128)(2,1)S(1)} %collective-permute-done.23.refs_7_), channel_id=1, source_target_pairs={{0,12},{4,0},{8,4},{12,8},{1,13},{5,1},{9,5},{13,9},{2,14},{6,2},{... | collective-permute-start | bytes 737288 | tf_op jit(solution)/shard_map/ppermute | solution.py:77
  138.2 8.4 %all-gather.4.cloned.1.call-done = bf16[32,4,40,640]{3,2,1,0:T(8,128)(2,1)} async-done(((bf16[1,4,40,640]{3,2,1,0:T(8,128)(2,1)}), bf16[32,4,40,640]{3,2,1,0:T(8,128)(2,1)}) %all-gather.4.cloned.1.call-update) | async-done | bytes 6553616 | tf_op jit(solution)/shard_map/all_gather | solution.py:522
  146.6 2.9 %copy-done.1 = bf16[32,4,40,640]{3,2,1,0:T(8,128)(2,1)S(1)} copy-done((bf16[32,4,40,640]{3,2,1,0:T(8,128)(2,1)S(1)}, bf16[32,4,40,640]{3,2,1,0:T(8,128)(2,1)}, u32[]{:S(2)}) %copy-start.1) | copy-done | bytes 6553624
  149.5 1.5 shard_map.175.refs_9_
  151.0 3.1 %shard_map.176 = bf16[2,4,96,320]{3,2,1,0:T(8,128)(2,1)S(1)} custom-call(s32[4]{0:T(128)S(1)} %copy-done.4, bf16[48,2560]{1,0:T(8,128)(2,1)S(1)} %copy-done.2, bf16[48,2560]{1,0:T(8,128)(2,1)S(1)} %collective-permute-done.19.refs_1_, bf16[48,2560]{1,0:T(8,128)(2,1)S(1)} %collective-permute-done.20.refs_2_, ...), custom_call_target="tpu_custom_call" | custom-call | flops 1258291200 | bytes 8000000 | tf_op jit(solution)/shard_map/pallas_call | solution.py:255
  154.2 1.0 collective-permute-start.26
  155.3 0.7 collective-permute-start.28
  155.9 7.6 %collective-permute-done.26.refs_10_ = bf16[4,96,320]{2,1,0:T(8,128)(2,1)S(1)} collective-permute-done((bf16[4,96,320]{2,1,0:T(8,128)(2,1)S(1)}, bf16[4,96,320]{2,1,0:T(8,128)(2,1)S(1)}, u32[]{:S(2)}, u32[]{:S(2)}) %collective-permute-start.26) | collective-permute-done | bytes 245792 | tf_op jit(solution)/shard_map/ppermute | solution.py:541
  163.5 2.9 %shard_map.177 = bf16[2,4,96,320]{3,2,1,0:T(8,128)(2,1)S(1)} custom-call(s32[4]{0:T(128)S(1)} %copy-done.4, bf16[48,2560]{1,0:T(8,128)(2,1)S(1)} %copy-done.2, bf16[48,2560]{1,0:T(8,128)(2,1)S(1)} %collective-permute-done.19.refs_1_, bf16[48,2560]{1,0:T(8,128)(2,1)S(1)} %collective-permute-done.20.refs_2_, ...), custom_call_target="tpu_custom_call" | custom-call | flops 1258291200 | bytes 8000000 | tf_op jit(solution)/shard_map/pallas_call | solution.py:255
  166.6 2.9 %collective-permute-done.28 = bf16[4,96,320]{2,1,0:T(8,128)(2,1)S(1)} collective-permute-done((bf16[4,96,320]{2,1,0:T(8,128)(2,1)S(1)}, bf16[4,96,320]{2,1,0:T(8,128)(2,1)S(1)}, u32[]{:S(2)}, u32[]{:S(2)}) %collective-permute-start.28) | collective-permute-done | bytes 245792 | tf_op jit(solution)/shard_map/ppermute | solution.py:541
  169.7 0.3 pad_maximum_fusion
  170.1 1.4 copy.52
  (83 shorter events, 2.3 us)
Async XLA Ops:
  7.2 84.3 %all-gather.6.cloned.1.call-start = ((), (), s32[]{:S(2)}) async-start(), calls=%async_computation.1 | async-start | bytes 4915200 | tf_op jit(solution)/shard_map/all_gather | solution.py:510
  9.1 3.2 %copy-start.14 = (f32[20,5120]{1,0:T(8,128)S(1)}, f32[20,5120]{1,0:T(8,128)}, u32[]{:S(2)}) copy-start(f32[20,5120]{1,0:T(8,128)} %param.17) | copy-start | bytes 1228804
  9.1 3.2 %copy-start.15 = (f32[20,5120]{1,0:T(8,128)S(1)}, f32[20,5120]{1,0:T(8,128)}, u32[]{:S(2)}) copy-start(f32[20,5120]{1,0:T(8,128)} %param.19) | copy-start | bytes 1228804
  9.2 13.2 %collective-permute-start.3 = (bf16[384,320]{1,0:T(8,128)(2,1)S(1)}, bf16[384,320]{1,0:T(8,128)(2,1)}, u32[]{:S(2)}, u32[]{:S(2)}) collective-permute-start(bf16[384,320]{1,0:T(8,128)(2,1)S(1)} %get-tuple-element.66), channel_id=1, source_target_pairs={{0,1},{1,0},{2,3},{3,2},{4,5},{5,4},{6,7},{7,6},{8,9},{9,8},{10,11... | collective-permute-start | bytes 737288 | tf_op jit(solution)/shard_map/ppermute | solution.py:478
  10.7 12.4 %collective-permute-start.5 = (bf16[384,320]{1,0:T(8,128)(2,1)S(1)}, bf16[384,320]{1,0:T(8,128)(2,1)}, u32[]{:S(2)}, u32[]{:S(2)}) collective-permute-start(bf16[384,320]{1,0:T(8,128)(2,1)S(1)} %get-tuple-element.64), channel_id=1, source_target_pairs={{0,3},{1,2},{2,1},{3,0},{4,7},{5,6},{6,5},{7,4},{8,11},{9,10},{10,... | collective-permute-start | bytes 737288 | tf_op jit(solution)/shard_map/ppermute | solution.py:478
  12.0 2.8 %copy-start.12 = (f32[40,3584]{1,0:T(8,128)S(1)}, f32[40,3584]{1,0:T(8,128)}, u32[]{:S(2)}) copy-start(f32[40,3584]{1,0:T(8,128)} %param.16) | copy-start | bytes 1720324
  12.0 2.8 %copy-start.13 = (f32[40,3584]{1,0:T(8,128)S(1)}, f32[40,3584]{1,0:T(8,128)}, u32[]{:S(2)}) copy-start(f32[40,3584]{1,0:T(8,128)} %param.18) | copy-start | bytes 1720324
  12.0 2.8 %copy-start.16 = (bf16[40,3584]{1,0:T(8,128)(2,1)S(1)}, bf16[40,3584]{1,0:T(8,128)(2,1)}, u32[]{:S(2)}) copy-start(bf16[40,3584]{1,0:T(8,128)(2,1)} %param.12) | copy-start | bytes 860164
  12.0 2.8 %copy-start.17 = (bf16[40,3584]{1,0:T(8,128)(2,1)S(1)}, bf16[40,3584]{1,0:T(8,128)(2,1)}, u32[]{:S(2)}) copy-start(bf16[40,3584]{1,0:T(8,128)(2,1)} %param.14) | copy-start | bytes 860164
  12.0 13.6 %collective-permute-start.4 = (bf16[384,320]{1,0:T(8,128)(2,1)S(1)}, bf16[384,320]{1,0:T(8,128)(2,1)}, u32[]{:S(2)}, u32[]{:S(2)}) collective-permute-start(bf16[384,320]{1,0:T(8,128)(2,1)S(1)} %get-tuple-element.65), channel_id=1, source_target_pairs={{0,2},{1,3},{2,0},{3,1},{4,6},{5,7},{6,4},{7,5},{8,10},{9,11},{10,... | collective-permute-start | bytes 737288 | tf_op jit(solution)/shard_map/ppermute | solution.py:478
  14.8 1.5 copy-start.11
  16.3 1.0 copy-start.10
  17.3 11.5 %collective-permute-start = (bf16[40,1536]{1,0:T(8,128)(2,1)}, bf16[40,1536]{1,0:T(8,128)(2,1)S(1)}, u32[]{:S(2)}, u32[]{:S(2)}) collective-permute-start(bf16[40,1536]{1,0:T(8,128)(2,1)} %get-tuple-element.71), channel_id=1, source_target_pairs={{0,4},{4,8},{8,12},{12,0},{1,5},{5,9},{9,13},{13,1},{2,6},{6,10},{... | collective-permute-start | bytes 368648 | tf_op jit(solution)/shard_map/ppermute | solution.py:77
  19.1 9.7 %collective-permute-start.1 = (bf16[40,1536]{1,0:T(8,128)(2,1)}, bf16[40,1536]{1,0:T(8,128)(2,1)}, u32[]{:S(2)}, u32[]{:S(2)}) collective-permute-start(bf16[40,1536]{1,0:T(8,128)(2,1)} %get-tuple-element.72), channel_id=1, source_target_pairs={{0,8},{4,12},{8,0},{12,4},{1,9},{5,13},{9,1},{13,5},{2,10},{6,14},... | collective-permute-start | bytes 368648 | tf_op jit(solution)/shard_map/ppermute | solution.py:77
  22.4 6.4 %collective-permute-start.2 = (bf16[40,1536]{1,0:T(8,128)(2,1)S(1)}, bf16[40,1536]{1,0:T(8,128)(2,1)S(1)}, u32[]{:S(2)}, u32[]{:S(2)}) collective-permute-start(bf16[40,1536]{1,0:T(8,128)(2,1)S(1)} %get-tuple-element.69), channel_id=1, source_target_pairs={{0,12},{4,0},{8,4},{12,8},{1,13},{5,1},{9,5},{13,9},{2,14},{6,2},{... | collective-permute-start | bytes 368648 | tf_op jit(solution)/shard_map/ppermute | solution.py:77
  28.8 0.7 copy-start.22
  28.8 0.7 copy-start.23
  31.4 13.5 %copy-start.18 = (bf16[4,40,896]{2,1,0:T(8,128)(2,1)S(1)}, bf16[4,40,896]{2,1,0:T(8,128)(2,1)}, u32[]{:S(2)}) copy-start(bf16[4,40,896]{2,1,0:T(8,128)(2,1)} %get-tuple-element.19) | copy-start | bytes 860164
  31.4 115.2 %all-gather.4.cloned.1.call-start = ((), (), s32[]{:S(2)}) async-start(), calls=%async_computation | async-start | bytes 6758400 | tf_op jit(solution)/shard_map/all_gather | solution.py:522
  31.5 9.9 %collective-permute-start.8 = (bf16[4,40,896]{2,1,0:T(8,128)(2,1)}, bf16[4,40,896]{2,1,0:T(8,128)(2,1)S(1)}, u32[]{:S(2)}, u32[]{:S(2)}) collective-permute-start(bf16[4,40,896]{2,1,0:T(8,128)(2,1)} %get-tuple-element.19), channel_id=1, source_target_pairs={{0,66},{1,49},{4,70},{5,53},{8,74},{9,57},{12,78},{13,61},{16,82},... | collective-permute-start | bytes 860168 | tf_op jit(solution)/shard_map/ppermute | solution.py:73
  34.4 7.5 %collective-permute-start.7 = (bf16[4,40,896]{2,1,0:T(8,128)(2,1)}, bf16[4,40,896]{2,1,0:T(8,128)(2,1)S(1)}, u32[]{:S(2)}, u32[]{:S(2)}) collective-permute-start(bf16[4,40,896]{2,1,0:T(8,128)(2,1)} %get-tuple-element.19), channel_id=1, source_target_pairs={{0,64},{1,33},{4,68},{5,37},{8,72},{9,41},{12,76},{13,45},{16,80},... | collective-permute-start | bytes 860168 | tf_op jit(solution)/shard_map/ppermute | solution.py:73
  34.7 10.2 %collective-permute-start.6 = (bf16[4,40,896]{2,1,0:T(8,128)(2,1)}, bf16[4,40,896]{2,1,0:T(8,128)(2,1)S(1)}, u32[]{:S(2)}, u32[]{:S(2)}) collective-permute-start(bf16[4,40,896]{2,1,0:T(8,128)(2,1)} %get-tuple-element.19), channel_id=1, source_target_pairs={{0,2},{1,17},{4,6},{5,21},{8,10},{9,25},{12,14},{13,29},{16,18},{1... | collective-permute-start | bytes 860168 | tf_op jit(solution)/shard_map/ppermute | solution.py:73
  45.1 38.2 %copy-start.5 = (bf16[4,4,40,896]{3,2,1,0:T(8,128)(2,1)}, bf16[4,4,40,896]{3,2,1,0:T(8,128)(2,1)S(1)}, u32[]{:S(2)}) copy-start(bf16[4,4,40,896]{3,2,1,0:T(8,128)(2,1)S(1)} %pad_maximum_fusion.1.refs_1_) | copy-start | bytes 3440644
  45.1 16.4 %collective-permute-start.9 = (bf16[4,4,40,896]{3,2,1,0:T(8,128)(2,1)S(1)}, bf16[4,4,40,896]{3,2,1,0:T(8,128)(2,1)S(1)}, u32[]{:S(2)}, u32[]{:S(2)}) collective-permute-start(bf16[4,4,40,896]{3,2,1,0:T(8,128)(2,1)S(1)} %pad_maximum_fusion.1.refs_1_), channel_id=1, source_target_pairs={{0,16},{1,3},{4,20},{5,7},{8,24},{9,11},{12,28},{13,15},{16,32},{1... | collective-permute-start | bytes 3440648 | tf_op jit(solution)/shard_map/ppermute | solution.py:73
  46.1 28.3 %collective-permute-start.10 = (bf16[4,4,40,896]{3,2,1,0:T(8,128)(2,1)S(1)}, bf16[4,4,40,896]{3,2,1,0:T(8,128)(2,1)S(1)}, u32[]{:S(2)}, u32[]{:S(2)}) collective-permute-start(bf16[4,4,40,896]{3,2,1,0:T(8,128)(2,1)S(1)} %pad_maximum_fusion.1.refs_1_), channel_id=1, source_target_pairs={{0,32},{1,65},{4,36},{5,69},{8,40},{9,73},{12,44},{13,77},{16,48},... | collective-permute-start | bytes 3440648 | tf_op jit(solution)/shard_map/ppermute | solution.py:73
  48.6 25.9 %collective-permute-start.11 = (bf16[4,4,40,896]{3,2,1,0:T(8,128)(2,1)S(1)}, bf16[4,4,40,896]{3,2,1,0:T(8,128)(2,1)}, u32[]{:S(2)}, u32[]{:S(2)}) collective-permute-start(bf16[4,4,40,896]{3,2,1,0:T(8,128)(2,1)S(1)} %pad_maximum_fusion.1.refs_1_), channel_id=1, source_target_pairs={{0,48},{1,67},{4,52},{5,71},{8,56},{9,75},{12,60},{13,79},{16,0},{... | collective-permute-start | bytes 3440648 | tf_op jit(solution)/shard_map/ppermute | solution.py:73
  61.5 12.9 %copy-start.6 = (bf16[4,4,40,896]{3,2,1,0:T(8,128)(2,1)}, bf16[4,4,40,896]{3,2,1,0:T(8,128)(2,1)S(1)}, u32[]{:S(2)}) copy-start(bf16[4,4,40,896]{3,2,1,0:T(8,128)(2,1)S(1)} %collective-permute-done.9.refs_2_.refs_0_) | copy-start | bytes 3440644
  74.4 1.0 copy-start.7
  75.4 9.0 %copy-start.24 = (s32[24]{0:T(128)S(1)}, s32[24]{0:T(128)}, u32[]{:S(2)}) copy-start(s32[24]{0:T(128)} %length_ref.1) | copy-start | bytes 292
  77.2 4.4 %collective-permute-start.25 = (bf16[4,20,640]{2,1,0:T(8,128)(2,1)}, bf16[4,20,640]{2,1,0:T(8,128)(2,1)S(1)}, u32[]{:S(2)}, u32[]{:S(2)}) collective-permute-start(bf16[4,20,640]{2,1,0:T(8,128)(2,1)} %get-tuple-element.28), channel_id=1, source_target_pairs={{0,1},{1,0},{2,3},{3,2},{4,5},{5,4},{6,7},{7,6},{8,9},{9,8},{10,11... | collective-permute-start | bytes 307208 | tf_op jit(solution)/shard_map/ppermute | solution.py:81
  83.4 3.0 %collective-permute-start.12 = (bf16[4,4,40,896]{3,2,1,0:T(8,128)(2,1)S(1)}, bf16[4,4,40,896]{3,2,1,0:T(8,128)(2,1)S(1)}, u32[]{:S(2)}, u32[]{:S(2)}) collective-permute-start(bf16[4,4,40,896]{3,2,1,0:T(8,128)(2,1)S(1)} %pad_maximum_fusion.1.refs_1_), channel_id=1, source_target_pairs={{0,1},{1,0},{2,3},{3,2},{4,5},{5,4},{6,7},{7,6},{8,9},{9,8},{10,11... | collective-permute-start | bytes 3440648 | tf_op jit(solution)/shard_map/ppermute | solution.py:81
  83.8 5.9 %collective-permute-start.13 = (bf16[4,4,40,896]{3,2,1,0:T(8,128)(2,1)}, bf16[4,4,40,896]{3,2,1,0:T(8,128)(2,1)S(1)}, u32[]{:S(2)}, u32[]{:S(2)}) collective-permute-start(bf16[4,4,40,896]{3,2,1,0:T(8,128)(2,1)} %copy-done.6), channel_id=1, source_target_pairs={{0,1},{1,0},{2,3},{3,2},{4,5},{5,4},{6,7},{7,6},{8,9},{9,8},{10,11... | collective-permute-start | bytes 3440648 | tf_op jit(solution)/shard_map/ppermute | solution.py:81
  83.9 5.9 %collective-permute-start.14 = (bf16[4,4,40,896]{3,2,1,0:T(8,128)(2,1)}, bf16[4,4,40,896]{3,2,1,0:T(8,128)(2,1)}, u32[]{:S(2)}, u32[]{:S(2)}) collective-permute-start(bf16[4,4,40,896]{3,2,1,0:T(8,128)(2,1)} %copy-done.7), channel_id=1, source_target_pairs={{0,1},{1,0},{2,3},{3,2},{4,5},{5,4},{6,7},{7,6},{8,9},{9,8},{10,11... | collective-permute-start | bytes 3440648 | tf_op jit(solution)/shard_map/ppermute | solution.py:81
  84.3 7.2 %collective-permute-start.15 = (bf16[4,4,40,896]{3,2,1,0:T(8,128)(2,1)}, bf16[4,4,40,896]{3,2,1,0:T(8,128)(2,1)}, u32[]{:S(2)}, u32[]{:S(2)}) collective-permute-start(bf16[4,4,40,896]{3,2,1,0:T(8,128)(2,1)} %collective-permute-done.11.refs_4_.refs_2_), channel_id=1, source_target_pairs={{0,1},{1,0},{2,3},{3,2},{4,5},{5,4},{6,7},{7,6},{8,9},{9,8},{10,11... | collective-permute-start | bytes 3440648 | tf_op jit(solution)/shard_map/ppermute | solution.py:81
  86.4 5.1 %copy-start.8 = (bf16[4,4,40,896]{3,2,1,0:T(8,128)(2,1)}, bf16[4,4,40,896]{3,2,1,0:T(8,128)(2,1)S(1)}, u32[]{:S(2)}) copy-start(bf16[4,4,40,896]{3,2,1,0:T(8,128)(2,1)S(1)} %collective-permute-done.12.refs_5_) | copy-start | bytes 3440644
  89.7 1.8 copy-start.9
  102.5 8.5 %collective-permute-start.16 = (bf16[96,896]{1,0:T(8,128)(2,1)}, bf16[96,896]{1,0:T(8,128)(2,1)S(1)}, u32[]{:S(2)}, u32[]{:S(2)}) collective-permute-start(bf16[96,896]{1,0:T(8,128)(2,1)} %get-tuple-element.21), channel_id=1, source_target_pairs={{0,4},{4,8},{8,12},{12,0},{1,5},{5,9},{9,13},{13,1},{2,6},{6,10},{... | collective-permute-start | bytes 516104 | tf_op jit(solution)/shard_map/ppermute | solution.py:77
  104.2 11.3 %collective-permute-start.17 = (bf16[96,896]{1,0:T(8,128)(2,1)}, bf16[96,896]{1,0:T(8,128)(2,1)S(1)}, u32[]{:S(2)}, u32[]{:S(2)}) collective-permute-start(bf16[96,896]{1,0:T(8,128)(2,1)} %get-tuple-element.22), channel_id=1, source_target_pairs={{0,8},{4,12},{8,0},{12,4},{1,9},{5,13},{9,1},{13,5},{2,10},{6,14},... | collective-permute-start | bytes 516104 | tf_op jit(solution)/shard_map/ppermute | solution.py:77
  107.5 8.0 %collective-permute-start.18 = (bf16[96,896]{1,0:T(8,128)(2,1)}, bf16[96,896]{1,0:T(8,128)(2,1)S(1)}, u32[]{:S(2)}, u32[]{:S(2)}) collective-permute-start(bf16[96,896]{1,0:T(8,128)(2,1)} %get-tuple-element.23), channel_id=1, source_target_pairs={{0,12},{4,0},{8,4},{12,8},{1,13},{5,1},{9,5},{13,9},{2,14},{6,2},{... | collective-permute-start | bytes 516104 | tf_op jit(solution)/shard_map/ppermute | solution.py:77
  111.0 4.6 %copy-start.19 = (bf16[96,896]{1,0:T(8,128)(2,1)}, bf16[96,896]{1,0:T(8,128)(2,1)S(1)}, u32[]{:S(2)}) copy-start(bf16[96,896]{1,0:T(8,128)(2,1)S(1)} %collective-permute-done.16.refs_1_) | copy-start | bytes 516100
  115.6 0.7 copy-start.20
  115.6 0.7 copy-start.21
  127.8 7.7 %collective-permute-start.19 = (bf16[48,2560]{1,0:T(8,128)(2,1)}, bf16[48,2560]{1,0:T(8,128)(2,1)S(1)}, u32[]{:S(2)}, u32[]{:S(2)}) collective-permute-start(bf16[48,2560]{1,0:T(8,128)(2,1)} %get-tuple-element.24.refs_0_), channel_id=1, source_target_pairs={{0,4},{4,8},{8,12},{12,0},{1,5},{5,9},{9,13},{13,1},{2,6},{6,10},{... | collective-permute-start | bytes 737288 | tf_op jit(solution)/shard_map/ppermute | solution.py:77
  128.9 6.9 %collective-permute-start.23 = (bf16[48,2560]{1,0:T(8,128)(2,1)}, bf16[48,2560]{1,0:T(8,128)(2,1)S(1)}, u32[]{:S(2)}, u32[]{:S(2)}) collective-permute-start(bf16[48,2560]{1,0:T(8,128)(2,1)} %get-tuple-element.25.refs_4_), channel_id=1, source_target_pairs={{0,12},{4,0},{8,4},{12,8},{1,13},{5,1},{9,5},{13,9},{2,14},{6,2},{... | collective-permute-start | bytes 737288 | tf_op jit(solution)/shard_map/ppermute | solution.py:77
  130.4 20.5 %collective-permute-start.21 = (bf16[48,2560]{1,0:T(8,128)(2,1)}, bf16[48,2560]{1,0:T(8,128)(2,1)S(1)}, u32[]{:S(2)}, u32[]{:S(2)}) collective-permute-start(bf16[48,2560]{1,0:T(8,128)(2,1)} %get-tuple-element.24.refs_0_), channel_id=1, source_target_pairs={{0,12},{4,0},{8,4},{12,8},{1,13},{5,1},{9,5},{13,9},{2,14},{6,2},{... | collective-permute-start | bytes 737288 | tf_op jit(solution)/shard_map/ppermute | solution.py:77
  131.7 19.3 %collective-permute-start.22 = (bf16[48,2560]{1,0:T(8,128)(2,1)}, bf16[48,2560]{1,0:T(8,128)(2,1)S(1)}, u32[]{:S(2)}, u32[]{:S(2)}) collective-permute-start(bf16[48,2560]{1,0:T(8,128)(2,1)} %get-tuple-element.25.refs_4_), channel_id=1, source_target_pairs={{0,4},{4,8},{8,12},{12,0},{1,5},{5,9},{9,13},{13,1},{2,6},{6,10},{... | collective-permute-start | bytes 737288 | tf_op jit(solution)/shard_map/ppermute | solution.py:77
  135.5 15.5 %collective-permute-start.20 = (bf16[48,2560]{1,0:T(8,128)(2,1)S(1)}, bf16[48,2560]{1,0:T(8,128)(2,1)S(1)}, u32[]{:S(2)}, u32[]{:S(2)}) collective-permute-start(bf16[48,2560]{1,0:T(8,128)(2,1)S(1)} %collective-permute-done.19.refs_1_), channel_id=1, source_target_pairs={{0,4},{4,8},{8,12},{12,0},{1,5},{5,9},{9,13},{13,1},{2,6},{6,10},{... | collective-permute-start | bytes 737288 | tf_op jit(solution)/shard_map/ppermute | solution.py:77
  135.8 15.2 %collective-permute-start.24 = (bf16[48,2560]{1,0:T(8,128)(2,1)S(1)}, bf16[48,2560]{1,0:T(8,128)(2,1)S(1)}, u32[]{:S(2)}, u32[]{:S(2)}) collective-permute-start(bf16[48,2560]{1,0:T(8,128)(2,1)S(1)} %collective-permute-done.23.refs_7_), channel_id=1, source_target_pairs={{0,12},{4,0},{8,4},{12,8},{1,13},{5,1},{9,5},{13,9},{2,14},{6,2},{... | collective-permute-start | bytes 737288 | tf_op jit(solution)/shard_map/ppermute | solution.py:77
  146.6 2.9 %copy-start.1 = (bf16[32,4,40,640]{3,2,1,0:T(8,128)(2,1)S(1)}, bf16[32,4,40,640]{3,2,1,0:T(8,128)(2,1)}, u32[]{:S(2)}) copy-start(bf16[32,4,40,640]{3,2,1,0:T(8,128)(2,1)} %all-gather.4.cloned.1.call-done) | copy-start | bytes 19660804
  149.5 1.5 copy-start
  149.5 1.5 copy-start.2
  149.5 1.6 copy-start.3
  149.5 1.6 copy-start.4
  154.2 9.3 %collective-permute-start.26 = (bf16[4,96,320]{2,1,0:T(8,128)(2,1)S(1)}, bf16[4,96,320]{2,1,0:T(8,128)(2,1)S(1)}, u32[]{:S(2)}, u32[]{:S(2)}) collective-permute-start(bf16[4,96,320]{2,1,0:T(8,128)(2,1)S(1)} %get-tuple-element.68), channel_id=1, source_target_pairs={{0,3},{1,2},{2,1},{3,0},{4,7},{5,6},{6,5},{7,4},{8,11},{9,10},{10,... | collective-permute-start | bytes 737288 | tf_op jit(solution)/shard_map/ppermute | solution.py:541
  155.3 14.2 %collective-permute-start.28 = (bf16[4,96,320]{2,1,0:T(8,128)(2,1)S(1)}, bf16[4,96,320]{2,1,0:T(8,128)(2,1)S(1)}, u32[]{:S(2)}, u32[]{:S(2)}) collective-permute-start(bf16[4,96,320]{2,1,0:T(8,128)(2,1)S(1)} %get-tuple-element.67), channel_id=1, source_target_pairs={{0,2},{1,3},{2,0},{3,1},{4,6},{5,7},{6,4},{7,5},{8,10},{9,11},{10,... | collective-permute-start | bytes 737288 | tf_op jit(solution)/shard_map/ppermute | solution.py:541
  166.5 3.0 %collective-permute-start.27 = (bf16[4,96,320]{2,1,0:T(8,128)(2,1)S(1)}, bf16[4,96,320]{2,1,0:T(8,128)(2,1)S(1)}, u32[]{:S(2)}, u32[]{:S(2)}) collective-permute-start(bf16[4,96,320]{2,1,0:T(8,128)(2,1)S(1)} %dynamic-slice_bitcast_fusion.1), channel_id=1, source_target_pairs={{0,1},{1,0},{2,3},{3,2},{4,5},{5,4},{6,7},{7,6},{8,9},{9,8},{10,11... | collective-permute-start | bytes 737288 | tf_op jit(solution)/shard_map/ppermute | solution.py:541
Sparse Core Ops, SparseCore 0:
  31.6 49.0 all-gather.5
  83.5 63.0 all-gather.3
